TPU v7x, 768 devices: a whole 4x8x12 slice. The times are simulated.
768 devices in a mesh: row: 64 (over y, x, core), col: 12 (over z).
Axes of the slice: x: 4, y: 8, z: 12, core: 2. Of those that a mesh axis runs over, the one named last changes fastest.
Arguments:
- sketch: float32 [196608, 128], P(('row', 'col')), may hold values from -6 to 6
- degrees: int32 [196608], P(('row', 'col')), may hold values from 1 to 2048, as said below
- tiles: bfloat16 [64, 12, 96, 128, 128], P('row', 'col'), may hold values from -6 to 6
- tile_rows: int32 [64, 12, 96], P('row', 'col'), may hold values from 0 to 23
- tile_peers: int32 [64, 12, 96], P('row', 'col'), may hold values from 0 to 63
- tile_counts: int32 [64, 12], P('row', 'col'), may hold values from 24 to 96, as said below
- requests: int32 [64, 12, 64], P('row', 'col'), may hold values from 0 to 1
Outputs:
- first_basis: float32 [196608, 128], P(('row', 'col'))
- embedding: float32 [196608, 128], P(('row', 'col'))
Inputs may be any that keep to these rules, and one draw needn't show every extreme that they name: `degrees`: degrees of every vertex; the largest is reached by some vertex. `tile_counts`: A device holds at most 96 live tiles, and some device holds exactly that many; slots from the count on are ignored. `requests`: every device reads exactly one panel block from every device with its index along col.
All inputs are finite; a program needn't handle non-finite values.
Results may differ from a plain program's by a relative error of at most 0.0042.
Values may be sent and summed in bfloat16 or wider, within the bound.
No kernel may reach another device: no remote copies, remote signals or barrier semaphores. Data moves between devices by JAX's collectives and lax.ppermute only.
A program may use at most 64 MiB of HBM per device.

v0:
```python
import jax
import jax.numpy as jnp
from jax import lax
from jax.sharding import PartitionSpec as P


def local_gram(image):
    return lax.dot_general(
        image,
        image,
        (((0,), (0,)), ((), ())),
        precision=lax.Precision.HIGHEST,
        preferred_element_type=jnp.float32,
    )


def on_device(sketch, degrees, tiles, tile_rows, tile_peers, tile_counts, requests):
    rows_dev = sketch.shape[0]
    sketch_width = sketch.shape[1]
    tile_edge = tiles.shape[-1]
    tile_slots = tiles.shape[2]
    row_devices = lax.axis_size("row")
    col_devices = lax.axis_size("col")
    blocks_dev = rows_dev // tile_edge
    group_blocks = col_devices * blocks_dev
    inverse_root = 1.0 / jnp.sqrt(degrees.astype(jnp.float32))
    own_tiles = tiles[0, 0]
    row_ids = tile_rows[0, 0]
    peer_ids = tile_peers[0, 0]
    live_count = tile_counts[0, 0]
    wanted = requests[0, 0]
    requested = lax.all_to_all(
        wanted.reshape(row_devices, 1), "row", split_axis=0, concat_axis=0, tiled=True
    ).reshape(row_devices)

    def fetch(panel):
        outgoing = panel.reshape(blocks_dev, tile_edge, sketch_width)[requested]
        arrived = lax.all_to_all(outgoing, "row", split_axis=0, concat_axis=0, tiled=True)
        return arrived[peer_ids]

    def product(panel):
        sources = fetch(panel)
        empty = jnp.zeros((group_blocks, tile_edge, sketch_width), jnp.float32)
        products = jnp.einsum(
            "tij,tjk->tik", own_tiles, sources, preferred_element_type=jnp.float32
        )
        active = (jnp.arange(tile_slots, dtype=jnp.int32) < live_count).astype(jnp.float32)
        summed = empty.at[row_ids].add(products * active[:, None, None])
        flat_term = summed.reshape(group_blocks * tile_edge, sketch_width)
        return (
            lax.psum_scatter(flat_term, "col", scatter_dimension=0, tiled=True)
            * inverse_root[:, None]
        )

    panel_one = (sketch * inverse_root[:, None]).astype(jnp.bfloat16)
    image_one = product(panel_one)
    gram_one = local_gram(image_one)
    gram_one = lax.psum(gram_one, ("row", "col"))
    panel_two = (image_one * inverse_root[:, None]).astype(jnp.bfloat16)
    image_two = product(panel_two)
    gram_two = local_gram(image_two)
    gram_two = lax.psum(gram_two, ("row", "col"))
    lower_one = jnp.linalg.cholesky(gram_one)
    mixed = jax.scipy.linalg.solve_triangular(lower_one, gram_two, lower=True)
    folded = jax.scipy.linalg.solve_triangular(lower_one, mixed.T, lower=True)
    folded = 0.5 * (folded + folded.T)
    lower_two = jnp.linalg.cholesky(folded)
    factor = jnp.sqrt(jnp.float32(rows_dev * row_devices * col_devices))
    first_basis = jax.scipy.linalg.solve_triangular(lower_one, image_one.T, lower=True).T * factor
    partial_solve = jax.scipy.linalg.solve_triangular(lower_one, image_two.T, lower=True)
    embedding = jax.scipy.linalg.solve_triangular(lower_two, partial_solve, lower=True).T * factor
    return (first_basis, embedding)


def solution(mesh):
    return jax.shard_map(
        on_device,
        mesh=mesh,
        in_specs=(
            P(("row", "col"), None),
            P(("row", "col")),
            P("row", "col", None, None, None),
            P("row", "col", None),
            P("row", "col", None),
            P("row", "col"),
            P("row", "col", None),
        ),
        out_specs=(P(("row", "col"), None), P(("row", "col"), None)),
        check_vma=False,
    )
```

profile of v0, /device:TPU:1, one launch (start us, length us, event | category | flops | bytes accessed | tf_op | source)
XLA Modules:
  0.0 873.2 jit_solution(12369883337192711528)
XLA Ops:
  7.2 1.5 copy.38
  8.7 14.5 %all-to-all-start = ((s32[64,1,1]{2,1,0:T(1,128)}), s32[64,1,1]{2,1,0:T(1,128)S(1)}, u32[]{:S(2)}, u32[]{:S(2)}) async-start(s32[64,1,1]{2,1,0:T(1,128)} %copy.38), calls=%async_computation | async-start | bytes 65536 | tf_op jit(solution)/shard_map/all_to_all | solution.py:32
  23.2 0.7 convert_rsqrt_fusion
  23.9 1.0 multiply_convert_fusion.1
  24.9 7.7 all-to-all-done
  32.6 1.2 reduce.4
  33.9 2.2 gather_fusion
  36.1 5.7 all-to-all-start.1
  41.8 0.0 reduce-scatter.3.cloned.1.call-start
  42.6 48.9 %all-to-all-done.1 = bf16[64,128,128]{2,1,0:T(8,128)(2,1)} async-done(((bf16[64,128,128]{2,1,0:T(8,128)(2,1)}), bf16[64,128,128]{2,1,0:T(8,128)(2,1)}, u32[]{:S(2)}, u32[]{:S(2)}) %all-to-all-start.1) | async-done | bytes 2097184 | tf_op jit(solution)/shard_map/all_to_all | solution.py:38
  91.4 4.3 gather_fusion.1
  95.7 6.9 multiply_bitcast_fusion.1
  102.6 6.6 copy.40
  109.2 1.3 broadcast.121.clone
  110.6 19.7 %scatter_fusion = f32[24,128,128]{2,1,0:T(8,128)} fusion(f32[24,128,128]{2,1,0:T(8,128)} %broadcast.121.clone, s32[96]{0:T(128)S(1)} %fusion.34, f32[96,128,128]{2,1,0:T(8,128)} %copy.40), kind=kCustom, calls=%fused_computation.4 | custom fusion | flops 1572864 | bytes 18874752 | tf_op jit(solution)/shard_map/scatter-add | solution.py:48
  130.3 0.0 reduce-scatter.5.cloned.1.call-start
  130.4 52.9 %reduce-scatter.3.cloned.1.call-done = f32[256,128]{1,0:T(8,128)} async-done(((f32[3072,128]{1,0:T(8,128)}), f32[256,128]{1,0:T(8,128)}) %reduce-scatter.3.cloned.1.call-update) | async-done | bytes 131088 | tf_op jit(solution)/shard_map/reduce_scatter | solution.py:51
  183.2 1.0 multiply_convert_fusion
  184.2 2.2 gather_fusion.2
  186.4 67.3 %all_to_all.22 = bf16[64,128,128]{2,1,0:T(8,128)(2,1)} all-to-all(bf16[64,128,128]{2,1,0:T(8,128)(2,1)} %gather_fusion.2), channel_id=1, replica_groups=mesh['row'=64,'col'=12] {'row'}, dimensions={0} | all-to-all | bytes 4194304 | tf_op jit(solution)/shard_map/all_to_all | solution.py:38
  253.7 4.3 gather_fusion.3
  258.0 6.9 multiply_bitcast_fusion
  264.9 6.6 copy.44
  271.5 1.3 broadcast.121
  272.9 19.7 %scatter_fusion.1 = f32[24,128,128]{2,1,0:T(8,128)} fusion(f32[24,128,128]{2,1,0:T(8,128)} %broadcast.121, s32[96]{0:T(128)S(1)} %fusion.34, f32[96,128,128]{2,1,0:T(8,128)} %copy.44), kind=kCustom, calls=%fused_computation.5 | custom fusion | flops 1572864 | bytes 18874752 | tf_op jit(solution)/shard_map/scatter-add | solution.py:48
  292.7 1.1 fusion.17
  293.8 46.1 %reduce-scatter.5.cloned.1.call-done = f32[256,128]{1,0:T(8,128)} async-done(((f32[3072,128]{1,0:T(8,128)}), f32[256,128]{1,0:T(8,128)}) %reduce-scatter.5.cloned.1.call-update) | async-done | bytes 131088 | tf_op jit(solution)/shard_map/reduce_scatter | solution.py:51
  340.0 2.1 fusion.14
  342.1 472.0 %all-reduce.3.cloned.1.call-done = (f32[128,128]{0,1:T(8,128)}, f32[128,128]{1,0:T(8,128)}) async-done(((f32[128,128]{0,1:T(8,128)}, f32[128,128]{1,0:T(8,128)}), (f32[128,128]{0,1:T(8,128)}, f32[128,128]{1,0:T(8,128)})) %all-reduce.3.cloned.1.call-update) | async-done | bytes 131088 | tf_op jit(solution)/shard_map/psum | solution.py:58
  814.1 0.9 copy.42
  815.0 0.9 fusion.29
  815.8 11.7 %cholesky.44 = f32[128,128]{1,0:T(8,128)S(1)} custom-call(f32[128,128]{1,0:T(8,128)S(1)} %fusion.29), custom_call_target="Cholesky" | custom-call | tf_op jit(solution)/shard_map/jit(cholesky)/cholesky | solution.py:63
  827.6 0.6 compare_reduce_fusion.1
  828.2 0.7 fusion.19
  828.9 9.8 %custom-call.11 = f32[1,128,128]{1,2,0:T(8,128)S(1)} custom-call(f32[1,128,128]{2,1,0:T(8,128)S(1)} %fusion.19), custom_call_target="InvertDiagBlocksLowerTriangular" | custom-call | tf_op jit(solution)/shard_map/jit(_solve_triangular)/triangular_solve | solution.py:69
  838.7 1.1 convolution_bitcast_fusion
  839.8 0.3 fusion.26
  840.1 0.1 copy.45
  840.2 0.1 copy.46
  840.4 11.7 %cholesky.55 = f32[128,128]{1,0:T(8,128)S(1)} custom-call(f32[128,128]{1,0:T(8,128)S(1)} %fusion.22), custom_call_target="Cholesky" | custom-call | tf_op jit(solution)/shard_map/jit(cholesky)/cholesky | solution.py:67
  852.1 0.6 compare_reduce_fusion
  852.8 0.7 fusion.20
  853.4 9.8 %custom-call.15 = f32[1,128,128]{1,2,0:T(8,128)S(1)} custom-call(f32[1,128,128]{2,1,0:T(8,128)S(1)} %fusion.20), custom_call_target="InvertDiagBlocksLowerTriangular" | custom-call | tf_op jit(solution)/shard_map/jit(_solve_triangular)/triangular_solve | solution.py:71
  863.2 1.3 fusion.10
  864.5 0.3 fusion.8
  864.8 0.8 copy.48
  865.6 0.4 fusion.9
  865.9 0.8 copy.47
  (22 shorter events, 0.2 us)
Async XLA Ops:
  7.2 88.6 %copy-start = (bf16[1,1,96,128,128]{4,3,2,1,0:T(8,128)(2,1)S(1)}, bf16[1,1,96,128,128]{4,3,2,1,0:T(8,128)(2,1)}, u32[]{:S(2)}) copy-start(bf16[1,1,96,128,128]{4,3,2,1,0:T(8,128)(2,1)} %param.14) | copy-start | bytes 9437188
  8.7 24.0 %all-to-all-start = ((s32[64,1,1]{2,1,0:T(1,128)}), s32[64,1,1]{2,1,0:T(1,128)S(1)}, u32[]{:S(2)}, u32[]{:S(2)}) async-start(s32[64,1,1]{2,1,0:T(1,128)} %copy.38), calls=%async_computation | async-start | bytes 65536 | tf_op jit(solution)/shard_map/all_to_all | solution.py:32
  36.1 6.4 copy-start.2
  36.1 6.5 copy-start.3
  36.1 55.3 %all-to-all-start.1 = ((bf16[64,128,128]{2,1,0:T(8,128)(2,1)}), bf16[64,128,128]{2,1,0:T(8,128)(2,1)}, u32[]{:S(2)}, u32[]{:S(2)}) async-start(bf16[64,128,128]{2,1,0:T(8,128)(2,1)} %gather_fusion), calls=%async_computation.1 | async-start | bytes 4194304 | tf_op jit(solution)/shard_map/all_to_all | solution.py:38
  41.8 141.4 %reduce-scatter.3.cloned.1.call-start = ((), (), s32[]{:S(2)}) async-start(), calls=%async_computation.5 | async-start | bytes 1703936 | tf_op jit(solution)/shard_map/reduce_scatter | solution.py:51
  130.3 209.6 %reduce-scatter.5.cloned.1.call-start = ((), (), s32[]{:S(2)}) async-start(), calls=%async_computation.6 | async-start | bytes 1703936 | tf_op jit(solution)/shard_map/reduce_scatter | solution.py:51
  272.9 19.8 %copy-start.1 = (f32[256,128]{1,0:T(8,128)S(1)}, f32[256,128]{1,0:T(8,128)}, u32[]{:S(2)}) copy-start(f32[256,128]{1,0:T(8,128)} %reduce-scatter.3.cloned.1.call-done) | copy-start | bytes 393220
  292.6 521.4 %all-reduce.3.cloned.1.call-start = ((), (), s32[]{:S(2)}) async-start(), calls=%async_computation.7 | async-start | bytes 262144 | tf_op jit(solution)/shard_map/psum | solution.py:58
Sparse Core Ops, SparseCore 0:
  130.4 52.7 reduce-scatter.2
  292.7 47.1 reduce-scatter.4
  346.3 467.6 all-reduce.2
where the time goes:
time: 875 us; the launch traced here: 873 us
  waiting for transfers between devices  628 us (72%)
  other arithmetic  90 us (10%)
  blocking collectives  67.3 us (8%)
  local copies, waits for them, and re-layouts  32.9 us (4%)
  starting transfers between devices  20.4 us (2%)
  matrix products  20.4 us (2%)
  between operations  14.6 us (2%)
    psum x1, waiting for transfers between devices, on_device(): gram_one = lax.psum(gram_one, ('row', 'col'))  472 us
    reduce_scatter x2, waiting for transfers between devices, product(): lax.psum_scatter(flat_term, 'col', scatter_dimension=0, tiled=True)  99 us
    all_to_all x1, blocking collectives, fetch(): lax.all_to_all(outgoing, 'row', split_axis=0, concat_axis=0, tiled=True)  67.3 us
    all_to_all x1, waiting for transfers between devices, fetch(): lax.all_to_all(outgoing, 'row', split_axis=0, concat_axis=0, tiled=True)  48.9 us
    scatter-add x2, other arithmetic, product(): summed = empty.at[row_ids].add(products * active[:, None, None])  39.5 us
  transfers between devices with their start and end apart: 5, of which 5 were waited for; matrix products, arithmetic and copies ran while one was open for 0% of the time, Pallas kernels for 0%

commit v1 on v0

v1 whole, which is shorter than its diff:
```python
import jax
import jax.numpy as jnp
from jax import lax
from jax.experimental import pallas as pl
from jax.experimental.pallas import tpu as pltpu
from jax.sharding import PartitionSpec as P

TILE = 128
EXTRA = 16
LEVELS = 32766.0
VMEM_LIMIT = 48 * 1024 * 1024


def diagonal_mask():
    return lax.broadcasted_iota(jnp.int32, (TILE, TILE), 0) == lax.broadcasted_iota(
        jnp.int32, (TILE, TILE), 1
    )


def to_lanes(column):
    return jnp.sum(jnp.where(diagonal_mask(), column, 0.0), axis=0, keepdims=True)


def to_sublanes(lanes):
    return jnp.sum(jnp.where(diagonal_mask(), lanes, 0.0), axis=1, keepdims=True)


def gram_of(image):
    return lax.dot_general(
        image,
        image,
        (((0,), (0,)), ((), ())),
        precision=lax.Precision.HIGHEST,
        preferred_element_type=jnp.float32,
    )


def write_requested(requested, panel, outgoing_ref):
    for peer in range(outgoing_ref.shape[0]):
        outgoing_ref[peer] = jnp.where(requested[peer] == 0, panel[:TILE], panel[TILE:])


def first_panel_kernel(requested, sketch_ref, root_ref, outgoing_ref):
    panel = (sketch_ref[...] * root_ref[...]).astype(jnp.bfloat16)
    write_requested(requested, panel, outgoing_ref)


def product_kernel(rows, sources, count, tiles_ref, arrived_ref, coded_ref, total):
    unroll = 8
    total[...] = jnp.zeros_like(total)

    def steps(group, carry):
        for k in range(unroll):
            slot = group * unroll + k
            row = rows[slot]
            total[row] += jnp.dot(
                tiles_ref[slot], arrived_ref[sources[slot]], preferred_element_type=jnp.float32
            )
        return carry

    lax.fori_loop(0, (count[0] + unroll - 1) // unroll, steps, 0)
    holders, coded_rows, _ = coded_ref.shape
    blocks = (coded_rows - EXTRA) // TILE
    line = lax.broadcasted_iota(jnp.int32, (EXTRA, TILE), 0)

    def code(holder, carry):
        exponents = jnp.zeros((EXTRA, TILE), jnp.float32)
        for b in range(blocks):
            value = total[holder * blocks + b]
            top = jnp.max(jnp.abs(value), axis=1, keepdims=True)
            exponent = jnp.ceil(jnp.log2(jnp.clip(top, 2.0**-100, 2.0**120)))
            scaled = value * (jnp.exp2(-exponent) * LEVELS)
            scaled = jnp.clip(jnp.floor(scaled + 0.5), -32767.0, 32767.0)
            coded_ref[holder, b * TILE : (b + 1) * TILE, :] = scaled.astype(jnp.int32).astype(jnp.int16)
            exponents = jnp.where(line == b, to_lanes(exponent), exponents)
        coded_ref[holder, blocks * TILE :, :] = exponents.astype(jnp.int32).astype(jnp.int16)
        return carry

    lax.fori_loop(0, holders, code, 0)


def decode(coded_ref, root_ref):
    holders, coded_rows, _ = coded_ref.shape
    blocks = (coded_rows - EXTRA) // TILE
    sums = [jnp.zeros((TILE, TILE), jnp.float32)] * blocks
    for holder in range(holders):
        exponents = coded_ref[holder, blocks * TILE :, :].astype(jnp.int32).astype(jnp.float32)
        for b in range(blocks):
            scale = jnp.exp2(to_sublanes(exponents[b : b + 1])) * (1.0 / LEVELS)
            value = coded_ref[holder, b * TILE : (b + 1) * TILE, :].astype(jnp.int32).astype(jnp.float32)
            sums[b] = sums[b] + value * scale
    return jnp.concatenate(sums, axis=0) * root_ref[...]


def middle_kernel(requested, coded_ref, root_ref, image_ref, gram_ref, outgoing_ref):
    image = decode(coded_ref, root_ref)
    image_ref[...] = image
    panel = (image * root_ref[...]).astype(jnp.bfloat16)
    write_requested(requested, panel, outgoing_ref)
    gram_ref[...] = gram_of(image)


def last_kernel(coded_ref, root_ref, image_ref, gram_ref):
    image = decode(coded_ref, root_ref)
    image_ref[...] = image
    gram_ref[...] = gram_of(image)


def call(kernel, out_shape, n_scalars, n_inputs, scratch=()):
    single = isinstance(out_shape, jax.ShapeDtypeStruct)
    return pl.pallas_call(
        kernel,
        out_shape=out_shape,
        in_specs=[pl.BlockSpec(memory_space=pltpu.SMEM)] * n_scalars
        + [pl.BlockSpec(memory_space=pltpu.VMEM)] * n_inputs,
        out_specs=pl.BlockSpec(memory_space=pltpu.VMEM)
        if single
        else [pl.BlockSpec(memory_space=pltpu.VMEM)] * len(out_shape),
        scratch_shapes=list(scratch),
        compiler_params=pltpu.CompilerParams(vmem_limit_bytes=VMEM_LIMIT),
    )


def sum_over_devices(value, row_devices, col_devices):
    rows, width = value.shape
    share = rows // row_devices
    parts = lax.all_to_all(
        value.reshape(row_devices, share, width), "row", split_axis=0, concat_axis=0, tiled=True
    )
    part = jnp.sum(parts, axis=0)
    parts = lax.all_to_all(
        jnp.broadcast_to(part[None], (col_devices, share, width)), "col", split_axis=0, concat_axis=0, tiled=True
    )
    part = jnp.sum(parts, axis=0)
    parts = lax.all_to_all(
        jnp.broadcast_to(part[None], (row_devices, share, width)), "row", split_axis=0, concat_axis=0, tiled=True
    )
    return parts.reshape(rows, width)


def on_device(sketch, degrees, tiles, tile_rows, tile_peers, tile_counts, requests):
    rows_dev, width = sketch.shape
    slots = tiles.shape[2]
    row_devices = lax.axis_size("row")
    col_devices = lax.axis_size("col")
    blocks_dev = rows_dev // TILE
    group_blocks = col_devices * blocks_dev
    f32, bf16, i16 = jnp.float32, jnp.bfloat16, jnp.int16
    shape = jax.ShapeDtypeStruct

    inverse_root = 1.0 / jnp.sqrt(degrees.astype(f32))
    root = jnp.broadcast_to(inverse_root[:, None], (rows_dev, width))
    own_tiles = tiles[0, 0]
    count = tile_counts[0]
    live = jnp.arange(slots, dtype=jnp.int32) < count
    row_ids = jnp.where(live, tile_rows[0, 0], group_blocks)
    source_ids = tile_peers[0, 0]
    requested = lax.all_to_all(
        requests[0, 0].reshape(row_devices, 1), "row", split_axis=0, concat_axis=0, tiled=True
    ).reshape(row_devices)

    outgoing_shape = shape((row_devices, TILE, width), bf16)
    coded_shape = shape((col_devices, rows_dev + EXTRA, width), i16)
    image_shape = shape((rows_dev, width), f32)
    gram_shape = shape((width, width), f32)
    total = pltpu.VMEM((group_blocks + 1, TILE, width), f32)

    def product(outgoing):
        arrived = lax.all_to_all(outgoing, "row", split_axis=0, concat_axis=0, tiled=True)
        coded = call(product_kernel, coded_shape, 3, 2, [total])(
            row_ids, source_ids, count, own_tiles, arrived
        )
        return lax.all_to_all(coded, "col", split_axis=0, concat_axis=0, tiled=True)

    outgoing = call(first_panel_kernel, outgoing_shape, 1, 2)(requested, sketch, root)
    terms = product(outgoing)
    image_one, gram_one, outgoing = call(
        middle_kernel, (image_shape, gram_shape, outgoing_shape), 1, 2
    )(requested, terms, root)
    terms = product(outgoing)
    image_two, gram_two = call(last_kernel, (image_shape, gram_shape), 0, 2)(terms, root)

    grams = sum_over_devices(jnp.concatenate([gram_one, gram_two], axis=1), row_devices, col_devices)
    gram_one, gram_two = grams[:, :width], grams[:, width:]
    lower_one = jnp.linalg.cholesky(gram_one)
    mixed = jax.scipy.linalg.solve_triangular(lower_one, gram_two, lower=True)
    folded = jax.scipy.linalg.solve_triangular(lower_one, mixed.T, lower=True)
    folded = 0.5 * (folded + folded.T)
    lower_two = jnp.linalg.cholesky(folded)
    factor = jnp.sqrt(f32(rows_dev * row_devices * col_devices))
    first_basis = jax.scipy.linalg.solve_triangular(lower_one, image_one.T, lower=True).T * factor
    partial_solve = jax.scipy.linalg.solve_triangular(lower_one, image_two.T, lower=True)
    embedding = jax.scipy.linalg.solve_triangular(lower_two, partial_solve, lower=True).T * factor
    return (first_basis, embedding)


def solution(mesh):
    return jax.shard_map(
        on_device,
        mesh=mesh,
        in_specs=(
            P(("row", "col"), None),
            P(("row", "col")),
            P("row", "col", None, None, None),
            P("row", "col", None),
            P("row", "col", None),
            P("row", "col"),
            P("row", "col", None),
        ),
        out_specs=(P(("row", "col"), None), P(("row", "col"), None)),
        check_vma=False,
    )
```

time: 875 us -> 337 us (0.39)
  waiting for transfers between devices: 628 us -> 57.7 us
  blocking collectives: 67.3 us -> 191 us
  other arithmetic: 90 us -> 47.8 us
  local copies, waits for them, and re-layouts: 32.9 us -> 5.65 us
  matrix products: 20.4 us -> 1.5 us
  between operations: 14.6 us -> 1.53 us
  Pallas kernels: 0 us -> 11.7 us
    psum x1 -> x0, waiting for transfers between devices: 472 us -> none  [on_device(): gram_one = lax.psum(gram_one, ('row', 'col'))]
    all_to_all x1 -> x6, blocking collectives: 67.3 us -> 191 us  [the longest x2 76 us: product(): return lax.all_to_all(coded, 'col', split_axis=0, concat_axis=0, tiled=True)]
    reduce_scatter x2 -> x0, waiting for transfers between devices: 99 us -> none  [product(): lax.psum_scatter(flat_term, 'col', scatter_dimension=0, tiled=True)]
    scatter-add x2 -> x0, other arithmetic: 39.5 us -> none  [product(): summed = empty.at[row_ids].add(products * active[:, None, None])]
    dot_general x4 -> x0, matrix products: 17.1 us -> none  [the longest x2 13.8 us: product(): jnp.einsum('tij,tjk->tik', own_tiles, sources, preferred_element_type=jnp...]
    mul x2 -> x0, local copies, waits for them, and re-layouts: 13.2 us -> none  [product(): summed = empty.at[row_ids].add(products * active[:, None, None])]
    gather x4 -> x0, local copies, waits for them, and re-layouts: 13 us -> none  [the longest x2 8.62 us: fetch(): return arrived[peer_ids]]
    pallas_call x0 -> x5, Pallas kernels: none -> 11.7 us  [the longest x2 8.56 us: product(): call(product_kernel, coded_shape, 3, 2, [total])]
  transfers between devices with their start and end apart: 5 -> 2, of which waited for: 5 -> 2; matrix products, arithmetic and copies ran while one was open for 0% -> 0% of each run, Pallas kernels for 0% -> 0%
where the time goes in v1:
time: 337 us
  blocking collectives  191 us (57%)
  waiting for transfers between devices  57.7 us (17%)
  other arithmetic  47.8 us (14%)
  starting transfers between devices  20.4 us (6%)
  Pallas kernels  11.7 us (3%)
  local copies, waits for them, and re-layouts  5.65 us (2%)
    all_to_all x2, blocking collectives, product(): return lax.all_to_all(coded, 'col', split_axis=0, concat_axis=0, tiled=True)  76 us
    all_to_all x1, blocking collectives, product(): lax.all_to_all(outgoing, 'row', split_axis=0, concat_axis=0, tiled=True)  61.7 us
    all_to_all x1, waiting for transfers between devices, product(): lax.all_to_all(outgoing, 'row', split_axis=0, concat_axis=0, tiled=True)  48.9 us
    all_to_all x1, blocking collectives, sum_over_devices(): lax.all_to_all(value.reshape(row_devices, share, width), 'row', split_axi...  25 us
    all_to_all x1, blocking collectives, sum_over_devices(): lax.all_to_all(jnp.broadcast_to(part[None], (row_devices, share, width)),...  16.1 us
    all_to_all x1, starting transfers between devices, on_device(): lax.all_to_all(requests[0, 0].reshape(row_devices, 1), 'row', split_axis=...  14.5 us
    another operation x3, other arithmetic, on_device(): lower_two = jnp.linalg.cholesky(folded)  12.4 us
    another operation x3, other arithmetic, on_device(): lower_one = jnp.linalg.cholesky(gram_one)  12.4 us
  transfers between devices with their start and end apart: 2, of which 2 were waited for; matrix products, arithmetic and copies ran while one was open for 0% of the time, Pallas kernels for 0%

profile of v1, /device:TPU:1, one launch (start us, length us, event | category | flops | bytes accessed | tf_op | source)
XLA Modules:
  0.0 336.8 jit_solution(12413997498206847339)
XLA Ops:
  0.6 1.4 copy.34
  2.0 14.5 %all-to-all-start = ((s32[64,1,1]{2,1,0:T(1,128)}), s32[64,1,1]{2,1,0:T(1,128)S(1)}, u32[]{:S(2)}, u32[]{:S(2)}) async-start(s32[64,1,1]{2,1,0:T(1,128)} %copy.34), calls=%async_computation | async-start | bytes 65536 | tf_op jit(solution)/shard_map/all_to_all | solution.py:158
  16.5 0.7 convert_rsqrt_fusion
  17.2 8.7 %all-to-all-done = s32[64,1,1]{2,1,0:T(1,128)S(1)} async-done(((s32[64,1,1]{2,1,0:T(1,128)}), s32[64,1,1]{2,1,0:T(1,128)S(1)}, u32[]{:S(2)}, u32[]{:S(2)}) %all-to-all-start) | async-done | bytes 288 | tf_op jit(solution)/shard_map/all_to_all | solution.py:158
  25.9 1.2 reduce.4.requested
  27.2 0.1 broadcast_in_dim.11.root_ref
  27.3 0.0 copy-start.2
  27.3 0.9 copy-done.2
  28.2 0.8 shard_map.86
  29.0 0.0 copy-start.1
  29.0 1.3 copy-done.1
  30.3 0.0 copy-start.4
  30.3 5.9 %all-to-all-start.1 = ((bf16[64,128,128]{2,1,0:T(8,128)(2,1)}), bf16[64,128,128]{2,1,0:T(8,128)(2,1)}, u32[]{:S(2)}, u32[]{:S(2)}) async-start(bf16[64,128,128]{2,1,0:T(8,128)(2,1)} %copy-done.1), calls=%async_computation.1 | async-start | bytes 4194304 | tf_op jit(solution)/shard_map/all_to_all | solution.py:169
  36.8 0.0 copy-done.4
  36.8 48.9 %all-to-all-done.1.arrived_ref = bf16[64,128,128]{2,1,0:T(8,128)(2,1)} async-done(((bf16[64,128,128]{2,1,0:T(8,128)(2,1)}), bf16[64,128,128]{2,1,0:T(8,128)(2,1)}, u32[]{:S(2)}, u32[]{:S(2)}) %all-to-all-start.1) | async-done | bytes 2097184 | tf_op jit(solution)/shard_map/all_to_all | solution.py:169
  85.8 0.0 copy-done
  85.8 0.0 copy-done.3
  85.8 4.8 %shard_map.87 = s16[12,272,128]{2,1,0:T(8,128)(2,1)S(1)} custom-call(s32[96]{0:T(128)S(1)} %compare_select_fusion.rows, s32[96]{0:T(128)S(1)} %bitcast.60, s32[1]{0:T(128)} %bitcast.56.count, bf16[96,128,128]{2,1,0:T(8,128)(2,1)S(1)} %bitcast.58, bf16[64,128,128]{2,1,0:T(8,128)(2,1)} %all-to-all-done.1.arrived_ref), custom_call_target="tpu_custom_call" | custom-call | tf_op jit(solution)/shard_map/pallas_call | solution.py:170
  90.6 43.5 %all_to_all.44.coded_ref = s16[12,272,128]{2,1,0:T(8,128)(2,1)S(1)} all-to-all(s16[12,272,128]{2,1,0:T(8,128)(2,1)S(1)} %shard_map.87), channel_id=1, replica_groups=mesh['row'=64,'col'=12] {'col'}, dimensions={0} | all-to-all | bytes 1671168 | tf_op jit(solution)/shard_map/all_to_all | solution.py:173
  134.1 1.6 shard_map.88
  135.7 61.7 %all_to_all.45.arrived_ref = bf16[64,128,128]{2,1,0:T(8,128)(2,1)S(1)} all-to-all(bf16[64,128,128]{2,1,0:T(8,128)(2,1)S(1)} %get-tuple-element.11), channel_id=1, replica_groups=mesh['row'=64,'col'=12] {'row'}, dimensions={0} | all-to-all | bytes 4194304 | tf_op jit(solution)/shard_map/all_to_all | solution.py:169
  197.3 3.8 %shard_map.89 = s16[12,272,128]{2,1,0:T(8,128)(2,1)S(1)} custom-call(s32[96]{0:T(128)S(1)} %compare_select_fusion.rows, s32[96]{0:T(128)S(1)} %bitcast.61, s32[1]{0:T(128)} %bitcast.57.count, bf16[96,128,128]{2,1,0:T(8,128)(2,1)S(1)} %bitcast.59, bf16[64,128,128]{2,1,0:T(8,128)(2,1)S(1)} %all_to_all.45.arrived_ref), custom_call_target="tpu_custom_call" | custom-call | tf_op jit(solution)/shard_map/pallas_call | solution.py:170
  201.1 32.6 %all_to_all.46.coded_ref = s16[12,272,128]{2,1,0:T(8,128)(2,1)S(1)} all-to-all(s16[12,272,128]{2,1,0:T(8,128)(2,1)S(1)} %shard_map.89), channel_id=1, replica_groups=mesh['row'=64,'col'=12] {'col'}, dimensions={0} | all-to-all | bytes 1671168 | tf_op jit(solution)/shard_map/all_to_all | solution.py:173
  233.7 0.8 shard_map.90
  234.5 0.1 reshape.33
  234.6 25.0 %all_to_all.47 = f32[64,2,256]{2,1,0:T(2,128)S(1)} all-to-all(f32[64,2,256]{2,1,0:T(2,128)S(1)} %reshape.33), channel_id=1, replica_groups=mesh['row'=64,'col'=12] {'row'}, dimensions={0} | all-to-all | bytes 262144 | tf_op jit(solution)/shard_map/all_to_all | solution.py:127
  259.5 0.1 reduce_sum.18
  259.6 11.8 %all_to_all.48 = f32[12,2,256]{2,1,0:T(2,128)S(1)} all-to-all(f32[12,2,256]{2,1,0:T(2,128)S(1)} %broadcast_in_dim.12), channel_id=1, replica_groups=mesh['row'=64,'col'=12] {'col'}, dimensions={0} | all-to-all | bytes 49152 | tf_op jit(solution)/shard_map/all_to_all | solution.py:131
  271.5 16.1 %all_to_all.49 = f32[64,2,256]{2,1,0:T(2,128)S(1)} all-to-all(f32[64,2,256]{2,1,0:T(2,128)S(1)} %broadcast_in_dim.13), channel_id=1, replica_groups=mesh['row'=64,'col'=12] {'row'}, dimensions={0} | all-to-all | bytes 262144 | tf_op jit(solution)/shard_map/all_to_all | solution.py:135
  287.6 0.1 reshape.34
  287.7 0.1 copy.41
  287.8 11.7 %cholesky.44 = f32[128,128]{1,0:T(8,128)S(1)} custom-call(f32[128,128]{1,0:T(8,128)S(1)} %fusion.16), custom_call_target="Cholesky" | custom-call | tf_op jit(solution)/shard_map/jit(cholesky)/cholesky | solution.py:185
  299.5 0.6 compare_reduce_fusion.1
  300.2 0.7 fusion.5
  300.8 9.8 %custom-call.11 = f32[1,128,128]{1,2,0:T(8,128)S(1)} custom-call(f32[1,128,128]{2,1,0:T(8,128)S(1)} %fusion.5), custom_call_target="InvertDiagBlocksLowerTriangular" | custom-call | tf_op jit(solution)/shard_map/jit(_solve_triangular)/triangular_solve | solution.py:191
  310.6 0.3 convolution_bitcast_fusion
  310.9 0.3 fusion.13
  311.2 0.3 fusion.2
  311.6 0.3 fusion.1
  311.9 0.8 copy.39
  312.6 0.1 copy.37
  312.7 0.1 copy.38
  312.9 11.7 %cholesky.55 = f32[128,128]{1,0:T(8,128)S(1)} custom-call(f32[128,128]{1,0:T(8,128)S(1)} %fusion.9), custom_call_target="Cholesky" | custom-call | tf_op jit(solution)/shard_map/jit(cholesky)/cholesky | solution.py:189
  324.6 0.6 compare_reduce_fusion
  325.2 0.7 fusion.6
  325.9 9.8 %custom-call.15 = f32[1,128,128]{1,2,0:T(8,128)S(1)} custom-call(f32[1,128,128]{2,1,0:T(8,128)S(1)} %fusion.6), custom_call_target="InvertDiagBlocksLowerTriangular" | custom-call | tf_op jit(solution)/shard_map/jit(_solve_triangular)/triangular_solve | solution.py:193
  335.7 0.3 fusion
  336.0 0.8 copy.40
  (13 shorter events, 0.2 us)
Async XLA Ops:
  2.0 24.0 %all-to-all-start = ((s32[64,1,1]{2,1,0:T(1,128)}), s32[64,1,1]{2,1,0:T(1,128)S(1)}, u32[]{:S(2)}, u32[]{:S(2)}) async-start(s32[64,1,1]{2,1,0:T(1,128)} %copy.34), calls=%async_computation | async-start | bytes 65536 | tf_op jit(solution)/shard_map/all_to_all | solution.py:158
  27.3 0.9 copy-start.2
  29.0 1.3 copy-start.1
  30.3 6.5 %copy-start.4 = (s32[1,1,96]{2,1,0:T(1,128)S(1)}, s32[1,1,96]{2,1,0:T(1,128)}, u32[]{:S(2)}) copy-start(s32[1,1,96]{2,1,0:T(1,128)} %param.15) | copy-start | bytes 1156
  30.3 55.5 %copy-start = (bf16[1,1,96,128,128]{4,3,2,1,0:T(8,128)(2,1)S(1)}, bf16[1,1,96,128,128]{4,3,2,1,0:T(8,128)(2,1)}, u32[]{:S(2)}) copy-start(bf16[1,1,96,128,128]{4,3,2,1,0:T(8,128)(2,1)} %param.14) | copy-start | bytes 9437188
  30.3 55.5 %copy-start.3 = (s32[1,1,96]{2,1,0:T(1,128)S(1)}, s32[1,1,96]{2,1,0:T(1,128)}, u32[]{:S(2)}) copy-start(s32[1,1,96]{2,1,0:T(1,128)} %param.16) | copy-start | bytes 1156
  30.3 55.5 %all-to-all-start.1 = ((bf16[64,128,128]{2,1,0:T(8,128)(2,1)}), bf16[64,128,128]{2,1,0:T(8,128)(2,1)}, u32[]{:S(2)}, u32[]{:S(2)}) async-start(bf16[64,128,128]{2,1,0:T(8,128)(2,1)} %copy-done.1), calls=%async_computation.1 | async-start | bytes 4194304 | tf_op jit(solution)/shard_map/all_to_all | solution.py:169

commit v2 on v1

v2 whole, which is shorter than its diff:
```python
import functools

import jax
import jax.numpy as jnp
from jax import lax
from jax.experimental import pallas as pl
from jax.experimental.pallas import tpu as pltpu
from jax.sharding import PartitionSpec as P

TILE = 128
EXTRA = 16
LEVELS = 32766.0
VMEM_LIMIT = 48 * 1024 * 1024
SUBLANES = 8
CORES = 2
CHIPS_X = 4
PLANE = CHIPS_X * CORES


def diagonal_mask():
    return lax.broadcasted_iota(jnp.int32, (TILE, TILE), 0) == lax.broadcasted_iota(
        jnp.int32, (TILE, TILE), 1
    )


def to_lanes(column):
    return jnp.sum(jnp.where(diagonal_mask(), column, 0.0), axis=0, keepdims=True)


def to_sublanes(lanes):
    return jnp.sum(jnp.where(diagonal_mask(), lanes, 0.0), axis=1, keepdims=True)


def write_copies(panel, copies_ref):
    for y in range(copies_ref.shape[0]):
        copies_ref[y] = panel


def first_panel_kernel(sketch_ref, root_ref, copies_ref):
    write_copies((sketch_ref[...] * root_ref[...]).astype(jnp.bfloat16), copies_ref)


def select_kernel(wanted, row, panels_ref, outgoing_ref):
    planes = panels_ref.shape[0]
    place = row[0] % PLANE
    x = place // CORES
    rows = planes * PLANE
    for g in range(PLANE):
        shift = (x - g // CORES + CHIPS_X) % CHIPS_X
        base = (shift * CORES + g % CORES) * rows + place
        for y in range(planes):
            outgoing_ref[g, y] = panels_ref[y, wanted[base + y * PLANE]]


def product_kernel(rows, peers, count, tiles_ref, arrived_ref, coded_ref, total):
    unroll = 8
    holders, coded_rows, _ = coded_ref.shape
    blocks = (coded_rows - EXTRA) // TILE
    spare = holders * blocks
    planes = arrived_ref.shape[0] // PLANE
    total[...] = jnp.zeros_like(total)

    def steps(group, carry):
        for k in range(unroll):
            slot = group * unroll + k
            row = jnp.where(slot < count[0], rows[slot], spare)
            peer = peers[slot]
            source = peer % PLANE * planes + peer // PLANE
            total[row] += jnp.dot(
                tiles_ref[slot], arrived_ref[source], preferred_element_type=jnp.float32
            )
        return carry

    lax.fori_loop(0, (count[0] + unroll - 1) // unroll, steps, 0)
    line = lax.broadcasted_iota(jnp.int32, (EXTRA, TILE), 0)
    for holder in range(holders):
        exponents = jnp.zeros((EXTRA, TILE), jnp.float32)
        for b in range(blocks):
            value = total[holder * blocks + b]
            top = jnp.max(jnp.abs(value), axis=1, keepdims=True)
            exponent = jnp.ceil(jnp.log2(jnp.clip(top, 2.0**-100, 2.0**120)))
            scaled = value * (jnp.exp2(-exponent) * LEVELS)
            scaled = jnp.clip(jnp.round(scaled), -32767.0, 32767.0)
            coded_ref[holder, b * TILE : (b + 1) * TILE, :] = scaled.astype(jnp.int32).astype(jnp.int16)
            exponents = jnp.where(line == b, to_lanes(exponent), exponents)
        coded_ref[holder, blocks * TILE :, :] = exponents.astype(jnp.int32).astype(jnp.int16)


def decode(coded_ref, root_ref):
    holders, coded_rows, _ = coded_ref.shape
    blocks = (coded_rows - EXTRA) // TILE
    sums = [jnp.zeros((TILE, TILE), jnp.float32)] * blocks
    for holder in range(holders):
        exponents = coded_ref[holder, blocks * TILE :, :].astype(jnp.int32).astype(jnp.float32)
        for b in range(blocks):
            scale = jnp.exp2(to_sublanes(exponents[b : b + 1])) * (1.0 / LEVELS)
            value = coded_ref[holder, b * TILE : (b + 1) * TILE, :].astype(jnp.int32).astype(jnp.float32)
            sums[b] = sums[b] + value * scale
    return jnp.concatenate(sums, axis=0) * root_ref[...]


def middle_kernel(coded_ref, root_ref, image_ref, gram_ref, copies_ref):
    image = decode(coded_ref, root_ref)
    image_ref[...] = image
    write_copies((image * root_ref[...]).astype(jnp.bfloat16), copies_ref)
    gram_ref[...] = dot(image, image, 0, 0)


def last_kernel(coded_ref, root_ref, image_ref, gram_ref):
    image = decode(coded_ref, root_ref)
    image_ref[...] = image
    gram_ref[...] = dot(image, image, 0, 0)


def dot(a, b, a_dim, b_dim):
    return lax.dot_general(
        a,
        b,
        (((a_dim,), (b_dim,)), ((), ())),
        precision=lax.Precision.HIGHEST,
        preferred_element_type=jnp.float32,
    )


def inverse_cholesky(gram):
    size = gram.shape[0]
    band = (SUBLANES, size)
    lane = lax.broadcasted_iota(jnp.int32, band, 1)
    line = lax.broadcasted_iota(jnp.int32, band, 0)
    steps = range(size // SUBLANES)
    inner = range(SUBLANES)
    left = [gram[SUBLANES * k : SUBLANES * (k + 1)] for k in steps]
    right = [(lane == line + SUBLANES * k).astype(jnp.float32) for k in steps]

    def spread(rows, column):
        return jnp.broadcast_to(rows[:, column : column + 1], band)

    for k in steps:
        start = SUBLANES * k
        row_left = [jnp.broadcast_to(left[k][j : j + 1], band) for j in inner]
        row_right = [jnp.broadcast_to(right[k][j : j + 1], band) for j in inner]
        entry = [[spread(row_left[j], start + t) if t >= j else None for t in inner] for j in inner]
        inverse = [None] * SUBLANES
        factor = [[None] * SUBLANES for _ in inner]
        for j in inner:
            inverse[j] = 1.0 / entry[j][j]
            for t in range(j + 1, SUBLANES):
                factor[t][j] = entry[j][t] * inverse[j]
                for u in range(t, SUBLANES):
                    entry[t][u] = entry[t][u] - factor[t][j] * entry[j][u]
                row_left[t] = row_left[t] - factor[t][j] * row_left[j]
                row_right[t] = row_right[t] - factor[t][j] * row_right[j]
        step_left = [row_left[j] * inverse[j] for j in inner]
        step_right = [row_right[j] * inverse[j] for j in inner]
        for q in steps[k + 1 :]:
            column = [spread(left[q], start + j) for j in inner]
            for j in inner:
                for t in range(j + 1, SUBLANES):
                    column[t] = column[t] - column[j] * factor[t][j]
            left[q] = left[q] - sum(column[j] * step_left[j] for j in inner)
            right[q] = right[q] - sum(column[j] * step_right[j] for j in inner)
        for j in inner:
            right[k] = jnp.where(line == j, row_right[j] * lax.rsqrt(entry[j][j]), right[k])
    return jnp.concatenate(right, axis=0)


def bases_kernel(scale, grams_ref, image_one_ref, image_two_ref, first_ref, second_ref):
    width = grams_ref.shape[0]
    inverse_one = inverse_cholesky(grams_ref[:, :width])
    partial_solve = dot(image_two_ref[...], inverse_one, 1, 1)
    first_ref[...] = dot(image_one_ref[...], inverse_one, 1, 1) * scale
    folded = dot(dot(inverse_one, grams_ref[:, width:], 1, 0), inverse_one, 1, 1)
    folded = 0.5 * (folded + folded.T)
    inverse_two = inverse_cholesky(folded)
    second_ref[...] = dot(partial_solve, inverse_two, 1, 1) * scale


def call(kernel, out_shape, n_scalars, n_inputs, scratch=()):
    single = isinstance(out_shape, jax.ShapeDtypeStruct)
    return pl.pallas_call(
        kernel,
        out_shape=out_shape,
        in_specs=[pl.BlockSpec(memory_space=pltpu.SMEM)] * n_scalars
        + [pl.BlockSpec(memory_space=pltpu.VMEM)] * n_inputs,
        out_specs=pl.BlockSpec(memory_space=pltpu.VMEM)
        if single
        else [pl.BlockSpec(memory_space=pltpu.VMEM)] * len(out_shape),
        scratch_shapes=list(scratch),
        compiler_params=pltpu.CompilerParams(vmem_limit_bytes=VMEM_LIMIT),
    )


def sum_over_devices(value, row_devices, col_devices):
    rows, width = value.shape
    share = rows // row_devices
    parts = lax.all_to_all(
        value.reshape(row_devices, share, width), "row", split_axis=0, concat_axis=0, tiled=True
    )
    part = jnp.sum(parts, axis=0)
    parts = lax.all_to_all(
        jnp.broadcast_to(part[None], (col_devices, share, width)), "col", split_axis=0, concat_axis=0, tiled=True
    )
    part = jnp.sum(parts, axis=0)
    parts = lax.all_to_all(
        jnp.broadcast_to(part[None], (row_devices, share, width)), "row", split_axis=0, concat_axis=0, tiled=True
    )
    return parts.reshape(rows, width)


def on_device(sketch, degrees, tiles, tile_rows, tile_peers, tile_counts, requests):
    rows_dev, width = sketch.shape
    row_devices = lax.axis_size("row")
    col_devices = lax.axis_size("col")
    blocks_dev = rows_dev // TILE
    group_blocks = col_devices * blocks_dev
    f32, bf16, i16 = jnp.float32, jnp.bfloat16, jnp.int16
    shape = jax.ShapeDtypeStruct

    inverse_root = 1.0 / jnp.sqrt(degrees.astype(f32))
    own_tiles = tiles[0, 0]
    count = tile_counts[0]
    planes = row_devices // PLANE
    row = lax.axis_index("row").reshape(1)

    mine = requests[0, 0]
    other = lax.ppermute(mine, "row", [(r, r ^ 1) for r in range(row_devices)])
    even = row[0] % CORES == 0
    pair = jnp.concatenate([jnp.where(even, mine, other), jnp.where(even, other, mine)])
    root = jnp.broadcast_to(inverse_root[:, None], (rows_dev, width))
    copies_shape = shape((planes, rows_dev, width), bf16)
    copies = call(first_panel_kernel, copies_shape, 0, 2)(sketch, root)
    pair, copies = lax.optimization_barrier((pair, copies))
    tables = [pair]
    for shift in range(1, CHIPS_X):
        tables.append(
            lax.ppermute(
                pair,
                "row",
                [
                    (r, r // PLANE * PLANE + (r + shift * CORES) % PLANE)
                    for r in range(row_devices)
                ],
            )
        )
    wanted = jnp.concatenate(tables)
    lines = [[y * PLANE + g for y in range(planes)] for g in range(PLANE)]
    plane = [[y * PLANE + g for g in range(PLANE)] for y in range(planes)]

    outgoing_shape = shape((PLANE, planes, TILE, width), bf16)
    coded_shape = shape((col_devices, rows_dev + EXTRA, width), i16)
    image_shape = shape((rows_dev, width), f32)
    gram_shape = shape((width, width), f32)
    total = pltpu.VMEM((group_blocks + 1, TILE, width), f32)

    def product(copies):
        panels = lax.all_to_all(
            copies, "row", split_axis=0, concat_axis=0, tiled=True, axis_index_groups=lines
        ).reshape(planes, blocks_dev, TILE, width)
        outgoing = call(select_kernel, outgoing_shape, 2, 1)(wanted, row, panels)
        arrived = lax.all_to_all(
            outgoing, "row", split_axis=0, concat_axis=0, tiled=True, axis_index_groups=plane
        ).reshape(row_devices, TILE, width)
        coded = call(product_kernel, coded_shape, 3, 2, [total])(
            tile_rows[0, 0], tile_peers[0, 0], count, own_tiles, arrived
        )
        return lax.all_to_all(coded, "col", split_axis=0, concat_axis=0, tiled=True)

    terms = product(copies)
    image_one, gram_one, copies = call(
        middle_kernel, (image_shape, gram_shape, copies_shape), 0, 2
    )(terms, root)
    terms = product(copies)
    image_two, gram_two = call(last_kernel, (image_shape, gram_shape), 0, 2)(terms, root)

    grams = sum_over_devices(jnp.concatenate([gram_one, gram_two], axis=1), row_devices, col_devices)
    scale = (rows_dev * row_devices * col_devices) ** 0.5
    return call(functools.partial(bases_kernel, scale), (image_shape, image_shape), 0, 3)(
        grams, image_one, image_two
    )


def solution(mesh):
    return jax.shard_map(
        on_device,
        mesh=mesh,
        in_specs=(
            P(("row", "col"), None),
            P(("row", "col")),
            P("row", "col", None, None, None),
            P("row", "col", None),
            P("row", "col", None),
            P("row", "col"),
            P("row", "col", None),
        ),
        out_specs=(P(("row", "col"), None), P(("row", "col"), None)),
        check_vma=False,
    )
```

time: 337 us -> 270 us (0.80)
  other arithmetic: 47.8 us -> 1.54 us
  waiting for transfers between devices: 57.7 us -> 36.5 us
  blocking collectives: 191 us -> 178 us
  Pallas kernels: 11.7 us -> 21.1 us
  starting transfers between devices: 20.4 us -> 28.1 us
    another operation x10 -> x0, other arithmetic: 45.7 us -> none  [the longest x3 12.4 us: on_device(): lower_two = jnp.linalg.cholesky(folded)]
    all_to_all x2, waiting for transfers between devices: 57.7 us -> 32.9 us  [the longest x1 25.8 us: product(): lax.all_to_all(outgoing, 'row', split_axis=0, concat_axis=0, tiled=True,...]
    ppermute x0 -> x4, starting transfers between devices: none -> 19.6 us  [the longest x1 12.4 us: on_device(): other = lax.ppermute(mine, 'row', [(r, r ^ 1) for r in range(row_devices)])]
    all_to_all x2, starting transfers between devices: 20.4 us -> 8.42 us  [the longest x1 4.93 us: product(): lax.all_to_all(outgoing, 'row', split_axis=0, concat_axis=0, tiled=True,...]
    pallas_call x2 -> x5, Pallas kernels: 2.41 us -> 14 us  [the longest x1 11 us: on_device(): call(functools.partial(bases_kernel, scale), (image_shape, image_shape),...]
    all_to_all x1 -> x2, blocking collectives: 61.7 us -> 50.5 us  [the longest x1 35 us: product(): lax.all_to_all(outgoing, 'row', split_axis=0, concat_axis=0, tiled=True,...]
    all_to_all x1, blocking collectives: 25 us -> 18.5 us  [sum_over_devices(): lax.all_to_all(value.reshape(row_devices, share, width), 'row', split_axi...]
    all_to_all x2, blocking collectives: 76 us -> 80.8 us  [product(): return lax.all_to_all(coded, 'col', split_axis=0, concat_axis=0, tiled=True)]
  transfers between devices with their start and end apart: 2 -> 6, of which waited for: 2 -> 3; matrix products, arithmetic and copies ran while one was open for 0% -> 0% of each run, Pallas kernels for 0% -> 0%
where the time goes in v2:
time: 270 us; the launch traced here: 269 us
  blocking collectives  178 us (66%)
  waiting for transfers between devices  36.5 us (14%)
  starting transfers between devices  28.1 us (10%)
  Pallas kernels  21.1 us (8%)
    all_to_all x2, blocking collectives, product(): return lax.all_to_all(coded, 'col', split_axis=0, concat_axis=0, tiled=True)  80.8 us
    all_to_all x1, blocking collectives, product(): lax.all_to_all(outgoing, 'row', split_axis=0, concat_axis=0, tiled=True,...  35 us
    all_to_all x1, waiting for transfers between devices, product(): lax.all_to_all(outgoing, 'row', split_axis=0, concat_axis=0, tiled=True,...  25.8 us
    all_to_all x1, blocking collectives, sum_over_devices(): lax.all_to_all(value.reshape(row_devices, share, width), 'row', split_axi...  18.5 us
    all_to_all x1, blocking collectives, sum_over_devices(): lax.all_to_all(jnp.broadcast_to(part[None], (row_devices, share, width)),...  16 us
    all_to_all x1, blocking collectives, product(): lax.all_to_all(copies, 'row', split_axis=0, concat_axis=0, tiled=True, ax...  15.5 us
    ppermute x1, starting transfers between devices, on_device(): other = lax.ppermute(mine, 'row', [(r, r ^ 1) for r in range(row_devices)])  12.4 us
    all_to_all x1, blocking collectives, sum_over_devices(): lax.all_to_all(jnp.broadcast_to(part[None], (col_devices, share, width)),...  11.8 us
  transfers between devices with their start and end apart: 6, of which 3 were waited for; matrix products, arithmetic and copies ran while one was open for 0% of the time, Pallas kernels for 0%

profile of v2, /device:TPU:1, one launch (start us, length us, event | category | flops | bytes accessed | tf_op | source)
XLA Modules:
  0.0 268.9 jit_solution(1361910062318474530)
XLA Ops:
  0.6 12.4 %collective-permute-start = (s32[64]{0:T(128)}, s32[64]{0:T(128)S(1)}, u32[]{:S(2)}, u32[]{:S(2)}) collective-permute-start(s32[64]{0:T(128)} %bitcast.23), channel_id=1, source_target_pairs={{0,12},{12,0},{24,36},{36,24},{48,60},{60,48},{72,84},{84,72},{96,... | collective-permute-start | bytes 776 | tf_op jit(solution)/shard_map/ppermute | solution.py:226
  13.1 0.7 convert_rsqrt_fusion
  13.8 0.1 broadcast_in_dim.6.root_ref
  13.9 0.0 copy-start.2
  13.9 0.9 copy-done.2
  14.8 0.8 shard_map.86
  15.6 0.0 collective-permute-done
  15.6 0.7 broadcast_select_fusion.1
  16.3 0.1 pad_add_fusion
  16.3 3.5 %all-to-all-start = ((bf16[8,256,128]{2,1,0:T(8,128)(2,1)}), bf16[8,256,128]{2,1,0:T(8,128)(2,1)S(1)}, u32[]{:S(2)}, u32[]{:S(2)}) async-start(bf16[8,256,128]{2,1,0:T(8,128)(2,1)} %shard_map.86), calls=%async_computation | async-start | bytes 1048576 | tf_op jit(solution)/shard_map/all_to_all | solution.py:256
  19.9 1.9 collective-permute-start.3
  21.8 1.9 collective-permute-start.2
  23.7 3.4 %collective-permute-start.1 = (s32[128]{0:T(128)S(1)}, s32[128]{0:T(128)S(1)}, u32[]{:S(2)}, u32[]{:S(2)}) collective-permute-start(s32[128]{0:T(128)S(1)} %pad_add_fusion), channel_id=1, source_target_pairs={{0,24},{12,36},{24,48},{36,60},{48,72},{60,84},{72,0},{84,12},{96,... | collective-permute-start | bytes 1544 | tf_op jit(solution)/shard_map/ppermute | solution.py:236
  27.1 3.6 %collective-permute-done.1 = s32[128]{0:T(128)S(1)} collective-permute-done((s32[128]{0:T(128)S(1)}, s32[128]{0:T(128)S(1)}, u32[]{:S(2)}, u32[]{:S(2)}) %collective-permute-start.1) | collective-permute-done | bytes 544 | tf_op jit(solution)/shard_map/ppermute | solution.py:236
  30.7 0.0 collective-permute-done.2
  30.7 0.0 collective-permute-done.3
  30.7 7.1 %all-to-all-done = bf16[8,256,128]{2,1,0:T(8,128)(2,1)S(1)} async-done(((bf16[8,256,128]{2,1,0:T(8,128)(2,1)}), bf16[8,256,128]{2,1,0:T(8,128)(2,1)S(1)}, u32[]{:S(2)}, u32[]{:S(2)}) %all-to-all-start) | async-done | bytes 524320 | tf_op jit(solution)/shard_map/all_to_all | solution.py:256
  37.8 0.7 shard_map.87
  38.5 0.0 copy-start.1
  38.6 1.3 copy-done.1
  39.9 0.0 copy-start
  39.9 0.0 copy-start.3
  39.9 0.0 copy-start.4
  39.9 4.9 %all-to-all-start.1 = ((bf16[8,8,128,128]{3,2,1,0:T(8,128)(2,1)}), bf16[8,8,128,128]{3,2,1,0:T(8,128)(2,1)}, u32[]{:S(2)}, u32[]{:S(2)}) async-start(bf16[8,8,128,128]{3,2,1,0:T(8,128)(2,1)} %copy-done.1), calls=%async_computation.1 | async-start | bytes 4194304 | tf_op jit(solution)/shard_map/all_to_all | solution.py:260
  45.5 25.8 %all-to-all-done.1 = bf16[8,8,128,128]{3,2,1,0:T(8,128)(2,1)} async-done(((bf16[8,8,128,128]{3,2,1,0:T(8,128)(2,1)}), bf16[8,8,128,128]{3,2,1,0:T(8,128)(2,1)}, u32[]{:S(2)}, u32[]{:S(2)}) %all-to-all-start.1) | async-done | bytes 2097184 | tf_op jit(solution)/shard_map/all_to_all | solution.py:260
  71.3 0.0 copy-done
  71.3 0.0 copy-done.3
  71.3 0.0 copy-done.4
  71.3 3.7 %shard_map.88 = s16[12,272,128]{2,1,0:T(8,128)(2,1)S(1)} custom-call(s32[96]{0:T(128)S(1)} %bitcast.19, s32[96]{0:T(128)S(1)} %bitcast.21, s32[1]{0:T(128)} %bitcast.12.count, bf16[96,128,128]{2,1,0:T(8,128)(2,1)S(1)} %bitcast.14, bf16[64,128,128]{2,1,0:T(8,128)(2,1)} %bitcast.7.arrived_ref), custom_call_target="tpu_custom_call" | custom-call | tf_op jit(solution)/shard_map/pallas_call | solution.py:263
  75.0 42.4 %all_to_all.45.coded_ref = s16[12,272,128]{2,1,0:T(8,128)(2,1)S(1)} all-to-all(s16[12,272,128]{2,1,0:T(8,128)(2,1)S(1)} %shard_map.88), channel_id=1, replica_groups=mesh['row'=64,'col'=12] {'col'}, dimensions={0} | all-to-all | bytes 1671168 | tf_op jit(solution)/shard_map/all_to_all | solution.py:266
  117.4 0.8 shard_map.89
  118.2 15.5 %all_to_all.46 = bf16[8,256,128]{2,1,0:T(8,128)(2,1)S(1)} all-to-all(bf16[8,256,128]{2,1,0:T(8,128)(2,1)S(1)} %get-tuple-element.12), channel_id=1, replica_groups={{0,96,192,288,384,480,576,672},{12,108,204,300,396,492,588,684},{24,120..., dimensions={0} | all-to-all | bytes 1048576 | tf_op jit(solution)/shard_map/all_to_all | solution.py:256
  133.8 0.7 shard_map.90
  134.5 35.0 %all_to_all.47 = bf16[8,8,128,128]{3,2,1,0:T(8,128)(2,1)S(1)} all-to-all(bf16[8,8,128,128]{3,2,1,0:T(8,128)(2,1)S(1)} %shard_map.90), channel_id=1, replica_groups={{0,12,24,36,48,60,72,84},{96,108,120,132,144,156,168,180},{192,204,216,..., dimensions={0} | all-to-all | bytes 4194304 | tf_op jit(solution)/shard_map/all_to_all | solution.py:260
  169.5 2.6 shard_map.91
  172.1 38.4 %all_to_all.48.coded_ref = s16[12,272,128]{2,1,0:T(8,128)(2,1)S(1)} all-to-all(s16[12,272,128]{2,1,0:T(8,128)(2,1)S(1)} %shard_map.91), channel_id=1, replica_groups=mesh['row'=64,'col'=12] {'col'}, dimensions={0} | all-to-all | bytes 1671168 | tf_op jit(solution)/shard_map/all_to_all | solution.py:266
  210.5 0.8 shard_map.92
  211.3 0.1 reshape.33
  211.4 18.5 %all_to_all.49 = f32[64,2,256]{2,1,0:T(2,128)S(1)} all-to-all(f32[64,2,256]{2,1,0:T(2,128)S(1)} %reshape.33), channel_id=1, replica_groups=mesh['row'=64,'col'=12] {'row'}, dimensions={0} | all-to-all | bytes 262144 | tf_op jit(solution)/shard_map/all_to_all | solution.py:196
  229.8 0.1 reduce_sum.18
  229.9 11.8 %all_to_all.50 = f32[12,2,256]{2,1,0:T(2,128)S(1)} all-to-all(f32[12,2,256]{2,1,0:T(2,128)S(1)} %broadcast_in_dim.7), channel_id=1, replica_groups=mesh['row'=64,'col'=12] {'col'}, dimensions={0} | all-to-all | bytes 49152 | tf_op jit(solution)/shard_map/all_to_all | solution.py:200
  241.8 16.0 %all_to_all.51 = f32[64,2,256]{2,1,0:T(2,128)S(1)} all-to-all(f32[64,2,256]{2,1,0:T(2,128)S(1)} %broadcast_in_dim.8), channel_id=1, replica_groups=mesh['row'=64,'col'=12] {'row'}, dimensions={0} | all-to-all | bytes 262144 | tf_op jit(solution)/shard_map/all_to_all | solution.py:204
  257.8 0.1 reshape.34.grams_ref
  257.9 11.0 %shard_map.93 = (f32[256,128]{1,0:T(8,128)}, f32[256,128]{1,0:T(8,128)}) custom-call(f32[128,256]{1,0:T(8,128)S(1)} %reshape.34.grams_ref, f32[256,128]{1,0:T(8,128)S(1)} %get-tuple-element.14.image_one_ref, f32[256,128]{1,0:T(8,128)S(1)} %get-tuple-element.15.image_two_ref), custom_call_target="tpu_custom_call" | custom-call | tf_op jit(solution)/shard_map/pallas_call | solution.py:277
  (9 shorter events, 0.1 us)
Async XLA Ops:
  0.6 15.0 %collective-permute-start = (s32[64]{0:T(128)}, s32[64]{0:T(128)S(1)}, u32[]{:S(2)}, u32[]{:S(2)}) collective-permute-start(s32[64]{0:T(128)} %bitcast.23), channel_id=1, source_target_pairs={{0,12},{12,0},{24,36},{36,24},{48,60},{60,48},{72,84},{84,72},{96,... | collective-permute-start | bytes 776 | tf_op jit(solution)/shard_map/ppermute | solution.py:226
  13.9 0.9 copy-start.2
  16.3 21.5 %all-to-all-start = ((bf16[8,256,128]{2,1,0:T(8,128)(2,1)}), bf16[8,256,128]{2,1,0:T(8,128)(2,1)S(1)}, u32[]{:S(2)}, u32[]{:S(2)}) async-start(bf16[8,256,128]{2,1,0:T(8,128)(2,1)} %shard_map.86), calls=%async_computation | async-start | bytes 1048576 | tf_op jit(solution)/shard_map/all_to_all | solution.py:256
  19.9 10.9 %collective-permute-start.3 = (s32[128]{0:T(128)S(1)}, s32[128]{0:T(128)S(1)}, u32[]{:S(2)}, u32[]{:S(2)}) collective-permute-start(s32[128]{0:T(128)S(1)} %pad_add_fusion), channel_id=1, source_target_pairs={{0,72},{12,84},{24,0},{36,12},{48,24},{60,36},{72,48},{84,60},{96,... | collective-permute-start | bytes 1544 | tf_op jit(solution)/shard_map/ppermute | solution.py:236
  21.8 8.9 %collective-permute-start.2 = (s32[128]{0:T(128)S(1)}, s32[128]{0:T(128)S(1)}, u32[]{:S(2)}, u32[]{:S(2)}) collective-permute-start(s32[128]{0:T(128)S(1)} %pad_add_fusion), channel_id=1, source_target_pairs={{0,48},{12,60},{24,72},{36,84},{48,0},{60,12},{72,24},{84,36},{96,... | collective-permute-start | bytes 1544 | tf_op jit(solution)/shard_map/ppermute | solution.py:236
  23.7 7.0 %collective-permute-start.1 = (s32[128]{0:T(128)S(1)}, s32[128]{0:T(128)S(1)}, u32[]{:S(2)}, u32[]{:S(2)}) collective-permute-start(s32[128]{0:T(128)S(1)} %pad_add_fusion), channel_id=1, source_target_pairs={{0,24},{12,36},{24,48},{36,60},{48,72},{60,84},{72,0},{84,12},{96,... | collective-permute-start | bytes 1544 | tf_op jit(solution)/shard_map/ppermute | solution.py:236
  38.5 1.3 copy-start.1
  39.9 31.4 %copy-start = (bf16[1,1,96,128,128]{4,3,2,1,0:T(8,128)(2,1)S(1)}, bf16[1,1,96,128,128]{4,3,2,1,0:T(8,128)(2,1)}, u32[]{:S(2)}) copy-start(bf16[1,1,96,128,128]{4,3,2,1,0:T(8,128)(2,1)} %param.9) | copy-start | bytes 9437188
  39.9 31.4 %copy-start.3 = (s32[1,1,96]{2,1,0:T(1,128)S(1)}, s32[1,1,96]{2,1,0:T(1,128)}, u32[]{:S(2)}) copy-start(s32[1,1,96]{2,1,0:T(1,128)} %param.10) | copy-start | bytes 1156
  39.9 31.4 %copy-start.4 = (s32[1,1,96]{2,1,0:T(1,128)S(1)}, s32[1,1,96]{2,1,0:T(1,128)}, u32[]{:S(2)}) copy-start(s32[1,1,96]{2,1,0:T(1,128)} %param.11) | copy-start | bytes 1156
  39.9 31.4 %all-to-all-start.1 = ((bf16[8,8,128,128]{3,2,1,0:T(8,128)(2,1)}), bf16[8,8,128,128]{3,2,1,0:T(8,128)(2,1)}, u32[]{:S(2)}, u32[]{:S(2)}) async-start(bf16[8,8,128,128]{3,2,1,0:T(8,128)(2,1)} %copy-done.1), calls=%async_computation.1 | async-start | bytes 4194304 | tf_op jit(solution)/shard_map/all_to_all | solution.py:260

commit v3 on v2

--- a/solution.py
+++ b/solution.py
@@ -36,8 +36,15 @@
         copies_ref[y] = panel
 
 
-def first_panel_kernel(sketch_ref, root_ref, copies_ref):
-    write_copies((sketch_ref[...] * root_ref[...]).astype(jnp.bfloat16), copies_ref)
+def first_panel_kernel(degrees_ref, sketch_ref, copies_ref, root_ref, sketch, arrival):
+    copy = pltpu.make_async_copy(sketch_ref, sketch, arrival)
+    copy.start()
+    roots = lax.rsqrt(degrees_ref[...].astype(jnp.float32))
+    for b in range(degrees_ref.shape[0]):
+        column = to_sublanes(roots[b : b + 1])
+        root_ref[b * TILE : (b + 1) * TILE] = jnp.broadcast_to(column, (TILE, root_ref.shape[1]))
+    copy.wait()
+    write_copies((sketch[...] * root_ref[...]).astype(jnp.bfloat16), copies_ref)
 
 
 def select_kernel(wanted, row, panels_ref, outgoing_ref):
@@ -47,13 +54,16 @@
     rows = planes * PLANE
     for g in range(PLANE):
         shift = (x - g // CORES + CHIPS_X) % CHIPS_X
-        base = (shift * CORES + g % CORES) * rows + place
+        side = (place + g) % CORES
+        base = (shift * CORES + side) * rows + place
         for y in range(planes):
             outgoing_ref[g, y] = panels_ref[y, wanted[base + y * PLANE]]
 
 
-def product_kernel(rows, peers, count, tiles_ref, arrived_ref, coded_ref, total):
-    unroll = 8
+def product_kernel(plan, tiles_ref, arrived_ref, coded_ref, total):
+    unroll = 32
+    slots = tiles_ref.shape[0]
+    count = plan[2 * slots]
     holders, coded_rows, _ = coded_ref.shape
     blocks = (coded_rows - EXTRA) // TILE
     spare = holders * blocks
@@ -63,15 +73,15 @@
     def steps(group, carry):
         for k in range(unroll):
             slot = group * unroll + k
-            row = jnp.where(slot < count[0], rows[slot], spare)
-            peer = peers[slot]
+            row = jnp.where(slot < count, plan[slot], spare)
+            peer = plan[slots + slot]
             source = peer % PLANE * planes + peer // PLANE
             total[row] += jnp.dot(
                 tiles_ref[slot], arrived_ref[source], preferred_element_type=jnp.float32
             )
         return carry
 
-    lax.fori_loop(0, (count[0] + unroll - 1) // unroll, steps, 0)
+    lax.fori_loop(0, (count + unroll - 1) // unroll, steps, 0)
     line = lax.broadcasted_iota(jnp.int32, (EXTRA, TILE), 0)
     for holder in range(holders):
         exponents = jnp.zeros((EXTRA, TILE), jnp.float32)
@@ -215,21 +225,24 @@
     group_blocks = col_devices * blocks_dev
     f32, bf16, i16 = jnp.float32, jnp.bfloat16, jnp.int16
     shape = jax.ShapeDtypeStruct
-
-    inverse_root = 1.0 / jnp.sqrt(degrees.astype(f32))
     own_tiles = tiles[0, 0]
-    count = tile_counts[0]
     planes = row_devices // PLANE
     row = lax.axis_index("row").reshape(1)
 
+    copies_shape = shape((planes, rows_dev, width), bf16)
+    image_shape = shape((rows_dev, width), f32)
+    copies, root = pl.pallas_call(
+        first_panel_kernel,
+        out_shape=(copies_shape, image_shape),
+        in_specs=[pl.BlockSpec(memory_space=pltpu.VMEM), pl.BlockSpec(memory_space=pl.ANY)],
+        out_specs=[pl.BlockSpec(memory_space=pltpu.VMEM)] * 2,
+        scratch_shapes=[pltpu.VMEM((rows_dev, width), f32), pltpu.SemaphoreType.DMA],
+        compiler_params=pltpu.CompilerParams(vmem_limit_bytes=VMEM_LIMIT),
+    )(degrees.reshape(blocks_dev, TILE), sketch)
+
     mine = requests[0, 0]
     other = lax.ppermute(mine, "row", [(r, r ^ 1) for r in range(row_devices)])
-    even = row[0] % CORES == 0
-    pair = jnp.concatenate([jnp.where(even, mine, other), jnp.where(even, other, mine)])
-    root = jnp.broadcast_to(inverse_root[:, None], (rows_dev, width))
-    copies_shape = shape((planes, rows_dev, width), bf16)
-    copies = call(first_panel_kernel, copies_shape, 0, 2)(sketch, root)
-    pair, copies = lax.optimization_barrier((pair, copies))
+    pair, copies = lax.optimization_barrier((jnp.concatenate([mine, other]), copies))
     tables = [pair]
     for shift in range(1, CHIPS_X):
         tables.append(
@@ -242,13 +255,17 @@
                 ],
             )
         )
-    wanted = jnp.concatenate(tables)
+    wanted, plan = lax.optimization_barrier(
+        (
+            jnp.concatenate(tables),
+            jnp.concatenate([tile_rows[0, 0], tile_peers[0, 0], tile_counts[0]]),
+        )
+    )
     lines = [[y * PLANE + g for y in range(planes)] for g in range(PLANE)]
     plane = [[y * PLANE + g for g in range(PLANE)] for y in range(planes)]
 
     outgoing_shape = shape((PLANE, planes, TILE, width), bf16)
     coded_shape = shape((col_devices, rows_dev + EXTRA, width), i16)
-    image_shape = shape((rows_dev, width), f32)
     gram_shape = shape((width, width), f32)
     total = pltpu.VMEM((group_blocks + 1, TILE, width), f32)
 
@@ -260,9 +277,7 @@
         arrived = lax.all_to_all(
             outgoing, "row", split_axis=0, concat_axis=0, tiled=True, axis_index_groups=plane
         ).reshape(row_devices, TILE, width)
-        coded = call(product_kernel, coded_shape, 3, 2, [total])(
-            tile_rows[0, 0], tile_peers[0, 0], count, own_tiles, arrived
-        )
+        coded = call(product_kernel, coded_shape, 1, 2, [total])(plan, own_tiles, arrived)
         return lax.all_to_all(coded, "col", split_axis=0, concat_axis=0, tiled=True)
 
     terms = product(copies)

time: 270 us -> 265 us (0.981)
  blocking collectives: 178 us -> 206 us
  waiting for transfers between devices: 36.5 us -> 9.34 us
  starting transfers between devices: 28.1 us -> 23.1 us
    all_to_all x1 -> x2, blocking collectives: 35 us -> 64.1 us  [product(): lax.all_to_all(outgoing, 'row', split_axis=0, concat_axis=0, tiled=True,...]
    all_to_all x1 -> x0, waiting for transfers between devices: 25.8 us -> none  [product(): lax.all_to_all(outgoing, 'row', split_axis=0, concat_axis=0, tiled=True,...]
    all_to_all x1 -> x0, starting transfers between devices: 4.93 us -> none  [product(): lax.all_to_all(outgoing, 'row', split_axis=0, concat_axis=0, tiled=True,...]
  transfers between devices with their start and end apart: 6 -> 5, of which waited for: 3 -> 2; matrix products, arithmetic and copies ran while one was open for 0% -> 0% of each run, Pallas kernels for 0% -> 0%
where the time goes in v3:
time: 265 us; the launch traced here: 264 us
  blocking collectives  206 us (78%)
  starting transfers between devices  23.1 us (9%)
  Pallas kernels  20.9 us (8%)
  waiting for transfers between devices  9.34 us (4%)
    all_to_all x2, blocking collectives, product(): return lax.all_to_all(coded, 'col', split_axis=0, concat_axis=0, tiled=True)  78.8 us
    all_to_all x2, blocking collectives, product(): lax.all_to_all(outgoing, 'row', split_axis=0, concat_axis=0, tiled=True,...  64.1 us
    all_to_all x1, blocking collectives, sum_over_devices(): lax.all_to_all(value.reshape(row_devices, share, width), 'row', split_axi...  18.4 us
    all_to_all x1, blocking collectives, product(): lax.all_to_all(copies, 'row', split_axis=0, concat_axis=0, tiled=True, ax...  16.9 us
    all_to_all x1, blocking collectives, sum_over_devices(): lax.all_to_all(jnp.broadcast_to(part[None], (row_devices, share, width)),...  16 us
    ppermute x1, starting transfers between devices, on_device(): other = lax.ppermute(mine, 'row', [(r, r ^ 1) for r in range(row_devices)])  12.4 us
    all_to_all x1, blocking collectives, sum_over_devices(): lax.all_to_all(jnp.broadcast_to(part[None], (col_devices, share, width)),...  11.8 us
    pallas_call x1, Pallas kernels, on_device(): call(functools.partial(bases_kernel, scale), (image_shape, image_shape),...  11 us
  transfers between devices with their start and end apart: 5, of which 2 were waited for; matrix products, arithmetic and copies ran while one was open for 0% of the time, Pallas kernels for 0%

profile of v3, /device:TPU:1, one launch (start us, length us, event | category | flops | bytes accessed | tf_op | source)
XLA Modules:
  0.0 264.1 jit_solution(8002542250850568108)
XLA Ops:
  0.6 12.4 %collective-permute-start = (s32[64]{0:T(128)}, s32[64]{0:T(128)S(1)}, u32[]{:S(2)}, u32[]{:S(2)}) collective-permute-start(s32[64]{0:T(128)} %bitcast.21), channel_id=1, source_target_pairs={{0,12},{12,0},{24,36},{36,24},{48,60},{60,48},{72,84},{84,72},{96,... | collective-permute-start | bytes 776 | tf_op jit(solution)/shard_map/ppermute | solution.py:244
  13.1 0.0 copy-start.1
  13.1 0.9 copy-done.1
  14.0 0.0 copy-start.2
  14.0 0.7 copy-done.2
  14.6 1.1 shard_map.86
  15.7 0.0 collective-permute-done
  15.8 0.7 pad_add_fusion.2
  16.5 3.5 %all-to-all-start = ((bf16[8,256,128]{2,1,0:T(8,128)(2,1)}), bf16[8,256,128]{2,1,0:T(8,128)(2,1)S(1)}, u32[]{:S(2)}, u32[]{:S(2)}) async-start(bf16[8,256,128]{2,1,0:T(8,128)(2,1)} %get-tuple-element.17), calls=%async_computation | async-start | bytes 1048576 | tf_op jit(solution)/shard_map/all_to_all | solution.py:273
  20.6 1.9 collective-permute-start.3
  22.6 1.9 collective-permute-start.2
  24.5 3.4 %collective-permute-start.1 = (s32[128]{0:T(128)S(1)}, s32[128]{0:T(128)S(1)}, u32[]{:S(2)}, u32[]{:S(2)}) collective-permute-start(s32[128]{0:T(128)S(1)} %pad_add_fusion.2), channel_id=1, source_target_pairs={{0,24},{12,36},{24,48},{36,60},{48,72},{60,84},{72,0},{84,12},{96,... | collective-permute-start | bytes 1544 | tf_op jit(solution)/shard_map/ppermute | solution.py:249
  27.9 0.7 pad_add_fusion.1.plan
  28.6 0.0 collective-permute-done.3
  28.6 0.0 collective-permute-done.2
  28.7 2.8 %collective-permute-done.1 = s32[128]{0:T(128)S(1)} collective-permute-done((s32[128]{0:T(128)S(1)}, s32[128]{0:T(128)S(1)}, u32[]{:S(2)}, u32[]{:S(2)}) %collective-permute-start.1) | collective-permute-done | bytes 544 | tf_op jit(solution)/shard_map/ppermute | solution.py:249
  31.5 6.5 %all-to-all-done = bf16[8,256,128]{2,1,0:T(8,128)(2,1)S(1)} async-done(((bf16[8,256,128]{2,1,0:T(8,128)(2,1)}), bf16[8,256,128]{2,1,0:T(8,128)(2,1)S(1)}, u32[]{:S(2)}, u32[]{:S(2)}) %all-to-all-start) | async-done | bytes 524320 | tf_op jit(solution)/shard_map/all_to_all | solution.py:273
  38.0 0.7 shard_map.87
  38.7 0.0 copy-start
  38.7 29.6 %all_to_all.45 = bf16[8,8,128,128]{3,2,1,0:T(8,128)(2,1)S(1)} all-to-all(bf16[8,8,128,128]{3,2,1,0:T(8,128)(2,1)S(1)} %shard_map.87), channel_id=1, replica_groups={{0,12,24,36,48,60,72,84},{96,108,120,132,144,156,168,180},{192,204,216,..., dimensions={0} | all-to-all | bytes 4194304 | tf_op jit(solution)/shard_map/all_to_all | solution.py:277
  68.3 0.0 copy-done
  68.3 2.9 %shard_map.88 = s16[12,272,128]{2,1,0:T(8,128)(2,1)S(1)} custom-call(s32[193]{0:T(256)S(1)} %pad_add_fusion.1.plan, bf16[96,128,128]{2,1,0:T(8,128)(2,1)S(1)} %bitcast.12, bf16[64,128,128]{2,1,0:T(8,128)(2,1)S(1)} %bitcast.15), custom_call_target="tpu_custom_call" | custom-call | tf_op jit(solution)/shard_map/pallas_call | solution.py:280
  71.2 41.0 %all_to_all.46.coded_ref = s16[12,272,128]{2,1,0:T(8,128)(2,1)S(1)} all-to-all(s16[12,272,128]{2,1,0:T(8,128)(2,1)S(1)} %shard_map.88), channel_id=1, replica_groups=mesh['row'=64,'col'=12] {'col'}, dimensions={0} | all-to-all | bytes 1671168 | tf_op jit(solution)/shard_map/all_to_all | solution.py:281
  112.2 0.8 shard_map.89
  113.0 16.9 %all_to_all.47 = bf16[8,256,128]{2,1,0:T(8,128)(2,1)S(1)} all-to-all(bf16[8,256,128]{2,1,0:T(8,128)(2,1)S(1)} %get-tuple-element.20), channel_id=1, replica_groups={{0,96,192,288,384,480,576,672},{12,108,204,300,396,492,588,684},{24,120..., dimensions={0} | all-to-all | bytes 1048576 | tf_op jit(solution)/shard_map/all_to_all | solution.py:273
  129.9 0.7 shard_map.90
  130.6 34.5 %all_to_all.48 = bf16[8,8,128,128]{3,2,1,0:T(8,128)(2,1)S(1)} all-to-all(bf16[8,8,128,128]{3,2,1,0:T(8,128)(2,1)S(1)} %shard_map.90), channel_id=1, replica_groups={{0,12,24,36,48,60,72,84},{96,108,120,132,144,156,168,180},{192,204,216,..., dimensions={0} | all-to-all | bytes 4194304 | tf_op jit(solution)/shard_map/all_to_all | solution.py:277
  165.1 2.9 %shard_map.91 = s16[12,272,128]{2,1,0:T(8,128)(2,1)S(1)} custom-call(s32[193]{0:T(256)S(1)} %pad_add_fusion.1.plan, bf16[96,128,128]{2,1,0:T(8,128)(2,1)S(1)} %bitcast.13, bf16[64,128,128]{2,1,0:T(8,128)(2,1)S(1)} %bitcast.14), custom_call_target="tpu_custom_call" | custom-call | tf_op jit(solution)/shard_map/pallas_call | solution.py:280
  168.0 37.8 %all_to_all.49.coded_ref = s16[12,272,128]{2,1,0:T(8,128)(2,1)S(1)} all-to-all(s16[12,272,128]{2,1,0:T(8,128)(2,1)S(1)} %shard_map.91), channel_id=1, replica_groups=mesh['row'=64,'col'=12] {'col'}, dimensions={0} | all-to-all | bytes 1671168 | tf_op jit(solution)/shard_map/all_to_all | solution.py:281
  205.8 0.8 shard_map.92
  206.6 0.1 reshape.36
  206.6 18.4 %all_to_all.50 = f32[64,2,256]{2,1,0:T(2,128)S(1)} all-to-all(f32[64,2,256]{2,1,0:T(2,128)S(1)} %reshape.36), channel_id=1, replica_groups=mesh['row'=64,'col'=12] {'row'}, dimensions={0} | all-to-all | bytes 262144 | tf_op jit(solution)/shard_map/all_to_all | solution.py:206
  225.1 0.1 reduce_sum.18
  225.2 11.8 %all_to_all.51 = f32[12,2,256]{2,1,0:T(2,128)S(1)} all-to-all(f32[12,2,256]{2,1,0:T(2,128)S(1)} %broadcast_in_dim.4), channel_id=1, replica_groups=mesh['row'=64,'col'=12] {'col'}, dimensions={0} | all-to-all | bytes 49152 | tf_op jit(solution)/shard_map/all_to_all | solution.py:210
  237.0 16.0 %all_to_all.52 = f32[64,2,256]{2,1,0:T(2,128)S(1)} all-to-all(f32[64,2,256]{2,1,0:T(2,128)S(1)} %broadcast_in_dim.5), channel_id=1, replica_groups=mesh['row'=64,'col'=12] {'row'}, dimensions={0} | all-to-all | bytes 262144 | tf_op jit(solution)/shard_map/all_to_all | solution.py:214
  253.1 0.1 reshape.37.grams_ref
  253.1 11.0 %shard_map.93 = (f32[256,128]{1,0:T(8,128)}, f32[256,128]{1,0:T(8,128)}) custom-call(f32[128,256]{1,0:T(8,128)S(1)} %reshape.37.grams_ref, f32[256,128]{1,0:T(8,128)S(1)} %get-tuple-element.22.image_one_ref, f32[256,128]{1,0:T(8,128)S(1)} %get-tuple-element.23.image_two_ref), custom_call_target="tpu_custom_call" | custom-call | tf_op jit(solution)/shard_map/pallas_call | solution.py:292
  (5 shorter events, 0.1 us)
Async XLA Ops:
  0.6 15.1 %collective-permute-start = (s32[64]{0:T(128)}, s32[64]{0:T(128)S(1)}, u32[]{:S(2)}, u32[]{:S(2)}) collective-permute-start(s32[64]{0:T(128)} %bitcast.21), channel_id=1, source_target_pairs={{0,12},{12,0},{24,36},{36,24},{48,60},{60,48},{72,84},{84,72},{96,... | collective-permute-start | bytes 776 | tf_op jit(solution)/shard_map/ppermute | solution.py:244
  13.1 0.9 copy-start.1
  14.0 0.7 copy-start.2
  16.5 21.5 %all-to-all-start = ((bf16[8,256,128]{2,1,0:T(8,128)(2,1)}), bf16[8,256,128]{2,1,0:T(8,128)(2,1)S(1)}, u32[]{:S(2)}, u32[]{:S(2)}) async-start(bf16[8,256,128]{2,1,0:T(8,128)(2,1)} %get-tuple-element.17), calls=%async_computation | async-start | bytes 1048576 | tf_op jit(solution)/shard_map/all_to_all | solution.py:273
  20.6 8.0 %collective-permute-start.3 = (s32[128]{0:T(128)S(1)}, s32[128]{0:T(128)S(1)}, u32[]{:S(2)}, u32[]{:S(2)}) collective-permute-start(s32[128]{0:T(128)S(1)} %pad_add_fusion.2), channel_id=1, source_target_pairs={{0,72},{12,84},{24,0},{36,12},{48,24},{60,36},{72,48},{84,60},{96,... | collective-permute-start | bytes 1544 | tf_op jit(solution)/shard_map/ppermute | solution.py:249
  22.6 6.1 %collective-permute-start.2 = (s32[128]{0:T(128)S(1)}, s32[128]{0:T(128)S(1)}, u32[]{:S(2)}, u32[]{:S(2)}) collective-permute-start(s32[128]{0:T(128)S(1)} %pad_add_fusion.2), channel_id=1, source_target_pairs={{0,48},{12,60},{24,72},{36,84},{48,0},{60,12},{72,24},{84,36},{96,... | collective-permute-start | bytes 1544 | tf_op jit(solution)/shard_map/ppermute | solution.py:249
  24.5 7.0 %collective-permute-start.1 = (s32[128]{0:T(128)S(1)}, s32[128]{0:T(128)S(1)}, u32[]{:S(2)}, u32[]{:S(2)}) collective-permute-start(s32[128]{0:T(128)S(1)} %pad_add_fusion.2), channel_id=1, source_target_pairs={{0,24},{12,36},{24,48},{36,60},{48,72},{60,84},{72,0},{84,12},{96,... | collective-permute-start | bytes 1544 | tf_op jit(solution)/shard_map/ppermute | solution.py:249
  38.7 29.6 %copy-start = (bf16[1,1,96,128,128]{4,3,2,1,0:T(8,128)(2,1)S(1)}, bf16[1,1,96,128,128]{4,3,2,1,0:T(8,128)(2,1)}, u32[]{:S(2)}) copy-start(bf16[1,1,96,128,128]{4,3,2,1,0:T(8,128)(2,1)} %param.9) | copy-start | bytes 9437188

commit v4 on v3

--- a/solution.py
+++ b/solution.py
@@ -140,38 +140,52 @@
     steps = range(size // SUBLANES)
     inner = range(SUBLANES)
     left = [gram[SUBLANES * k : SUBLANES * (k + 1)] for k in steps]
-    right = [(lane == line + SUBLANES * k).astype(jnp.float32) for k in steps]
+    result = []
 
     def spread(rows, column):
         return jnp.broadcast_to(rows[:, column : column + 1], band)
 
     for k in steps:
         start = SUBLANES * k
-        row_left = [jnp.broadcast_to(left[k][j : j + 1], band) for j in inner]
-        row_right = [jnp.broadcast_to(right[k][j : j + 1], band) for j in inner]
-        entry = [[spread(row_left[j], start + t) if t >= j else None for t in inner] for j in inner]
-        inverse = [None] * SUBLANES
-        factor = [[None] * SUBLANES for _ in inner]
-        for j in inner:
-            inverse[j] = 1.0 / entry[j][j]
-            for t in range(j + 1, SUBLANES):
-                factor[t][j] = entry[j][t] * inverse[j]
+        cleared = (lane >= start) & (lane < start + SUBLANES)
+        columns = [spread(left[k], start + t) for t in inner]
+        entry = [[jnp.broadcast_to(columns[t][j : j + 1], band) if t >= j else None for t in inner] for j in inner]
+        own = jnp.where(cleared, (lane == line + start).astype(jnp.float32), left[k])
+        row = [jnp.broadcast_to(own[j : j + 1], band) for j in inner]
+        factor = {}
+        solved = [None] * SUBLANES
+        final = [None] * SUBLANES
+        for j in range(0, SUBLANES, 2):
+            a, b, c = entry[j][j], entry[j][j + 1], entry[j + 1][j + 1]
+            over = 1.0 / (a * c - b * b)
+            rest = range(j + 2, SUBLANES)
+            first = {t: c * entry[j][t] - b * entry[j + 1][t] for t in rest}
+            second = {t: a * entry[j + 1][t] - b * entry[j][t] for t in rest}
+            for t in rest:
                 for u in range(t, SUBLANES):
-                    entry[t][u] = entry[t][u] - factor[t][j] * entry[j][u]
-                row_left[t] = row_left[t] - factor[t][j] * row_left[j]
-                row_right[t] = row_right[t] - factor[t][j] * row_right[j]
-        step_left = [row_left[j] * inverse[j] for j in inner]
-        step_right = [row_right[j] * inverse[j] for j in inner]
+                    entry[t][u] = entry[t][u] - (first[t] * entry[j][u] + second[t] * entry[j + 1][u]) * over
+            for t in rest:
+                factor[t, j], factor[t, j + 1] = first[t] * over, second[t] * over
+                row[t] = row[t] - (factor[t, j] * row[j] + factor[t, j + 1] * row[j + 1])
+            solved[j] = (c * row[j] - b * row[j + 1]) * over
+            solved[j + 1] = (a * row[j + 1] - b * row[j]) * over
+            ratio = b * (1.0 / a)
+            final[j] = row[j] * lax.rsqrt(a)
+            final[j + 1] = (row[j + 1] - ratio * row[j]) * lax.rsqrt(c - b * ratio)
+        rows = final[0]
+        for j in range(1, SUBLANES):
+            rows = jnp.where(line == j, final[j], rows)
+        result.append(jnp.where(lane < start + SUBLANES, rows, 0.0))
         for q in steps[k + 1 :]:
             column = [spread(left[q], start + j) for j in inner]
-            for j in inner:
-                for t in range(j + 1, SUBLANES):
-                    column[t] = column[t] - column[j] * factor[t][j]
-            left[q] = left[q] - sum(column[j] * step_left[j] for j in inner)
-            right[q] = right[q] - sum(column[j] * step_right[j] for j in inner)
-        for j in inner:
-            right[k] = jnp.where(line == j, row_right[j] * lax.rsqrt(entry[j][j]), right[k])
-    return jnp.concatenate(right, axis=0)
+            for j in range(0, SUBLANES, 2):
+                for t in range(j + 2, SUBLANES):
+                    column[t] = column[t] - (factor[t, j] * column[j] + factor[t, j + 1] * column[j + 1])
+            terms = [column[j] * solved[j] for j in inner]
+            while len(terms) > 1:
+                terms = [terms[i] + terms[i + 1] for i in range(0, len(terms), 2)]
+            left[q] = jnp.where(cleared, 0.0, left[q]) - terms[0]
+    return jnp.concatenate(result, axis=0)
 
 
 def bases_kernel(scale, grams_ref, image_one_ref, image_two_ref, first_ref, second_ref):
@@ -242,7 +256,7 @@
 
     mine = requests[0, 0]
     other = lax.ppermute(mine, "row", [(r, r ^ 1) for r in range(row_devices)])
-    pair, copies = lax.optimization_barrier((jnp.concatenate([mine, other]), copies))
+    pair = jnp.concatenate([mine, other])
     tables = [pair]
     for shift in range(1, CHIPS_X):
         tables.append(

time: 265 us -> 264 us (level)
  waiting for transfers between devices: 9.34 us -> 2.83 us
  blocking collectives: 206 us -> 212 us
    all_to_all x1, waiting for transfers between devices: 6.5 us -> 0.01 us  [product(): lax.all_to_all(copies, 'row', split_axis=0, concat_axis=0, tiled=True, ax...]
    all_to_all x1, blocking collectives: 16.9 us -> 21.5 us  [product(): lax.all_to_all(copies, 'row', split_axis=0, concat_axis=0, tiled=True, ax...]
    all_to_all x1, starting transfers between devices: 3.49 us -> 7.66 us  [product(): lax.all_to_all(copies, 'row', split_axis=0, concat_axis=0, tiled=True, ax...]
    ppermute x1, starting transfers between devices: 12.4 us -> 8.28 us  [on_device(): other = lax.ppermute(mine, 'row', [(r, r ^ 1) for r in range(row_devices)])]
  transfers between devices with their start and end apart: 5 -> 5, of which waited for: 2 -> 2; matrix products, arithmetic and copies ran while one was open for 0% -> 1% of each run, Pallas kernels for 0% -> 0%
where the time goes in v4:
time: 264 us; the launch traced here: 263 us
  blocking collectives  212 us (80%)
  starting transfers between devices  23.1 us (9%)
  Pallas kernels  19.6 us (7%)
  waiting for transfers between devices  2.83 us (1%)
    all_to_all x2, blocking collectives, product(): return lax.all_to_all(coded, 'col', split_axis=0, concat_axis=0, tiled=True)  78.6 us
    all_to_all x2, blocking collectives, product(): lax.all_to_all(outgoing, 'row', split_axis=0, concat_axis=0, tiled=True,...  65.9 us
    all_to_all x1, blocking collectives, product(): lax.all_to_all(copies, 'row', split_axis=0, concat_axis=0, tiled=True, ax...  21.5 us
    all_to_all x1, blocking collectives, sum_over_devices(): lax.all_to_all(value.reshape(row_devices, share, width), 'row', split_axi...  18.5 us
    all_to_all x1, blocking collectives, sum_over_devices(): lax.all_to_all(jnp.broadcast_to(part[None], (row_devices, share, width)),...  16 us
    all_to_all x1, blocking collectives, sum_over_devices(): lax.all_to_all(jnp.broadcast_to(part[None], (col_devices, share, width)),...  11.8 us
    pallas_call x1, Pallas kernels, on_device(): call(functools.partial(bases_kernel, scale), (image_shape, image_shape),...  9.71 us
    ppermute x1, starting transfers between devices, on_device(): other = lax.ppermute(mine, 'row', [(r, r ^ 1) for r in range(row_devices)])  8.28 us
  transfers between devices with their start and end apart: 5, of which 2 were waited for; matrix products, arithmetic and copies ran while one was open for 1% of the time, Pallas kernels for 0%

profile of v4, /device:TPU:1, one launch (start us, length us, event | category | flops | bytes accessed | tf_op | source)
XLA Modules:
  0.0 263.4 jit_solution(8524082992383286163)
XLA Ops:
  0.6 0.0 copy-start.1
  0.6 0.9 copy-done.1
  1.5 0.0 copy-start.2
  1.5 0.7 copy-done.2
  2.2 1.1 shard_map.86
  3.3 7.7 %all-to-all-start = ((bf16[8,256,128]{2,1,0:T(8,128)(2,1)}), bf16[8,256,128]{2,1,0:T(8,128)(2,1)S(1)}, u32[]{:S(2)}, u32[]{:S(2)}) async-start(bf16[8,256,128]{2,1,0:T(8,128)(2,1)} %get-tuple-element.13), calls=%async_computation | async-start | bytes 1048576 | tf_op jit(solution)/shard_map/all_to_all | solution.py:287
  11.0 8.3 %collective-permute-start = (s32[64]{0:T(128)}, s32[64]{0:T(128)S(1)}, u32[]{:S(2)}, u32[]{:S(2)}) collective-permute-start(s32[64]{0:T(128)} %bitcast.21), channel_id=1, source_target_pairs={{0,12},{12,0},{24,36},{36,24},{48,60},{60,48},{72,84},{84,72},{96,... | collective-permute-start | bytes 776 | tf_op jit(solution)/shard_map/ppermute | solution.py:258
  19.9 0.3 collective-permute-done
  20.2 0.7 pad_add_fusion.1
  20.9 1.9 collective-permute-start.3
  22.8 1.9 collective-permute-start.2
  24.8 3.4 %collective-permute-start.1 = (s32[128]{0:T(128)S(1)}, s32[128]{0:T(128)S(1)}, u32[]{:S(2)}, u32[]{:S(2)}) collective-permute-start(s32[128]{0:T(128)S(1)} %pad_add_fusion.1), channel_id=1, source_target_pairs={{0,24},{12,36},{24,48},{36,60},{48,72},{60,84},{72,0},{84,12},{96,... | collective-permute-start | bytes 1544 | tf_op jit(solution)/shard_map/ppermute | solution.py:263
  28.1 0.8 pad_add_fusion.plan
  28.9 0.0 collective-permute-done.3
  28.9 0.0 collective-permute-done.2
  28.9 2.5 collective-permute-done.1
  31.4 0.7 concatenate.14.wanted
  32.2 0.0 all-to-all-done
  32.2 0.7 shard_map.87
  32.9 0.0 copy-start
  32.9 31.6 %all_to_all.45 = bf16[8,8,128,128]{3,2,1,0:T(8,128)(2,1)S(1)} all-to-all(bf16[8,8,128,128]{3,2,1,0:T(8,128)(2,1)S(1)} %shard_map.87), channel_id=1, replica_groups={{0,12,24,36,48,60,72,84},{96,108,120,132,144,156,168,180},{192,204,216,..., dimensions={0} | all-to-all | bytes 4194304 | tf_op jit(solution)/shard_map/all_to_all | solution.py:291
  64.5 0.0 copy-done
  64.5 2.9 %shard_map.88 = s16[12,272,128]{2,1,0:T(8,128)(2,1)S(1)} custom-call(s32[193]{0:T(256)S(1)} %pad_add_fusion.plan, bf16[96,128,128]{2,1,0:T(8,128)(2,1)S(1)} %bitcast.12, bf16[64,128,128]{2,1,0:T(8,128)(2,1)S(1)} %bitcast.15), custom_call_target="tpu_custom_call" | custom-call | tf_op jit(solution)/shard_map/pallas_call | solution.py:294
  67.4 41.5 %all_to_all.46.coded_ref = s16[12,272,128]{2,1,0:T(8,128)(2,1)S(1)} all-to-all(s16[12,272,128]{2,1,0:T(8,128)(2,1)S(1)} %shard_map.88), channel_id=1, replica_groups=mesh['row'=64,'col'=12] {'col'}, dimensions={0} | all-to-all | bytes 1671168 | tf_op jit(solution)/shard_map/all_to_all | solution.py:295
  108.9 0.8 shard_map.89
  109.7 21.5 %all_to_all.47 = bf16[8,256,128]{2,1,0:T(8,128)(2,1)S(1)} all-to-all(bf16[8,256,128]{2,1,0:T(8,128)(2,1)S(1)} %get-tuple-element.16), channel_id=1, replica_groups={{0,96,192,288,384,480,576,672},{12,108,204,300,396,492,588,684},{24,120..., dimensions={0} | all-to-all | bytes 1048576 | tf_op jit(solution)/shard_map/all_to_all | solution.py:287
  131.2 0.7 shard_map.90
  131.9 34.3 %all_to_all.48 = bf16[8,8,128,128]{3,2,1,0:T(8,128)(2,1)S(1)} all-to-all(bf16[8,8,128,128]{3,2,1,0:T(8,128)(2,1)S(1)} %shard_map.90), channel_id=1, replica_groups={{0,12,24,36,48,60,72,84},{96,108,120,132,144,156,168,180},{192,204,216,..., dimensions={0} | all-to-all | bytes 4194304 | tf_op jit(solution)/shard_map/all_to_all | solution.py:291
  166.3 2.9 %shard_map.91 = s16[12,272,128]{2,1,0:T(8,128)(2,1)S(1)} custom-call(s32[193]{0:T(256)S(1)} %pad_add_fusion.plan, bf16[96,128,128]{2,1,0:T(8,128)(2,1)S(1)} %bitcast.13, bf16[64,128,128]{2,1,0:T(8,128)(2,1)S(1)} %bitcast.14), custom_call_target="tpu_custom_call" | custom-call | tf_op jit(solution)/shard_map/pallas_call | solution.py:294
  169.2 37.1 %all_to_all.49.coded_ref = s16[12,272,128]{2,1,0:T(8,128)(2,1)S(1)} all-to-all(s16[12,272,128]{2,1,0:T(8,128)(2,1)S(1)} %shard_map.91), channel_id=1, replica_groups=mesh['row'=64,'col'=12] {'col'}, dimensions={0} | all-to-all | bytes 1671168 | tf_op jit(solution)/shard_map/all_to_all | solution.py:295
  206.2 0.8 shard_map.92
  207.0 0.1 reshape.36
  207.1 18.5 %all_to_all.50 = f32[64,2,256]{2,1,0:T(2,128)S(1)} all-to-all(f32[64,2,256]{2,1,0:T(2,128)S(1)} %reshape.36), channel_id=1, replica_groups=mesh['row'=64,'col'=12] {'row'}, dimensions={0} | all-to-all | bytes 262144 | tf_op jit(solution)/shard_map/all_to_all | solution.py:220
  225.6 0.1 reduce_sum.18
  225.7 11.8 %all_to_all.51 = f32[12,2,256]{2,1,0:T(2,128)S(1)} all-to-all(f32[12,2,256]{2,1,0:T(2,128)S(1)} %broadcast_in_dim.4), channel_id=1, replica_groups=mesh['row'=64,'col'=12] {'col'}, dimensions={0} | all-to-all | bytes 49152 | tf_op jit(solution)/shard_map/all_to_all | solution.py:224
  237.6 16.0 %all_to_all.52 = f32[64,2,256]{2,1,0:T(2,128)S(1)} all-to-all(f32[64,2,256]{2,1,0:T(2,128)S(1)} %broadcast_in_dim.5), channel_id=1, replica_groups=mesh['row'=64,'col'=12] {'row'}, dimensions={0} | all-to-all | bytes 262144 | tf_op jit(solution)/shard_map/all_to_all | solution.py:228
  253.6 0.1 reshape.37.grams_ref
  253.7 9.7 %shard_map.93 = (f32[256,128]{1,0:T(8,128)}, f32[256,128]{1,0:T(8,128)}) custom-call(f32[128,256]{1,0:T(8,128)S(1)} %reshape.37.grams_ref, f32[256,128]{1,0:T(8,128)S(1)} %get-tuple-element.18.image_one_ref, f32[256,128]{1,0:T(8,128)S(1)} %get-tuple-element.19.image_two_ref), custom_call_target="tpu_custom_call" | custom-call | tf_op jit(solution)/shard_map/pallas_call | solution.py:306
  (4 shorter events, 0.1 us)
Async XLA Ops:
  0.6 0.9 copy-start.1
  1.5 0.7 copy-start.2
  3.3 28.9 %all-to-all-start = ((bf16[8,256,128]{2,1,0:T(8,128)(2,1)}), bf16[8,256,128]{2,1,0:T(8,128)(2,1)S(1)}, u32[]{:S(2)}, u32[]{:S(2)}) async-start(bf16[8,256,128]{2,1,0:T(8,128)(2,1)} %get-tuple-element.13), calls=%async_computation | async-start | bytes 1048576 | tf_op jit(solution)/shard_map/all_to_all | solution.py:287
  11.0 9.2 %collective-permute-start = (s32[64]{0:T(128)}, s32[64]{0:T(128)S(1)}, u32[]{:S(2)}, u32[]{:S(2)}) collective-permute-start(s32[64]{0:T(128)} %bitcast.21), channel_id=1, source_target_pairs={{0,12},{12,0},{24,36},{36,24},{48,60},{60,48},{72,84},{84,72},{96,... | collective-permute-start | bytes 776 | tf_op jit(solution)/shard_map/ppermute | solution.py:258
  20.9 8.0 %collective-permute-start.3 = (s32[128]{0:T(128)S(1)}, s32[128]{0:T(128)S(1)}, u32[]{:S(2)}, u32[]{:S(2)}) collective-permute-start(s32[128]{0:T(128)S(1)} %pad_add_fusion.1), channel_id=1, source_target_pairs={{0,72},{12,84},{24,0},{36,12},{48,24},{60,36},{72,48},{84,60},{96,... | collective-permute-start | bytes 1544 | tf_op jit(solution)/shard_map/ppermute | solution.py:263
  22.8 6.1 %collective-permute-start.2 = (s32[128]{0:T(128)S(1)}, s32[128]{0:T(128)S(1)}, u32[]{:S(2)}, u32[]{:S(2)}) collective-permute-start(s32[128]{0:T(128)S(1)} %pad_add_fusion.1), channel_id=1, source_target_pairs={{0,48},{12,60},{24,72},{36,84},{48,0},{60,12},{72,24},{84,36},{96,... | collective-permute-start | bytes 1544 | tf_op jit(solution)/shard_map/ppermute | solution.py:263
  24.8 6.7 %collective-permute-start.1 = (s32[128]{0:T(128)S(1)}, s32[128]{0:T(128)S(1)}, u32[]{:S(2)}, u32[]{:S(2)}) collective-permute-start(s32[128]{0:T(128)S(1)} %pad_add_fusion.1), channel_id=1, source_target_pairs={{0,24},{12,36},{24,48},{36,60},{48,72},{60,84},{72,0},{84,12},{96,... | collective-permute-start | bytes 1544 | tf_op jit(solution)/shard_map/ppermute | solution.py:263
  32.9 31.6 %copy-start = (bf16[1,1,96,128,128]{4,3,2,1,0:T(8,128)(2,1)S(1)}, bf16[1,1,96,128,128]{4,3,2,1,0:T(8,128)(2,1)}, u32[]{:S(2)}) copy-start(bf16[1,1,96,128,128]{4,3,2,1,0:T(8,128)(2,1)} %param.9) | copy-start | bytes 9437188

commit v5 on v3

--- a/solution.py
+++ b/solution.py
@@ -87,12 +87,16 @@
         exponents = jnp.zeros((EXTRA, TILE), jnp.float32)
         for b in range(blocks):
             value = total[holder * blocks + b]
+            top = jnp.max(jnp.abs(value), axis=0, keepdims=True)
+            column = jnp.ceil(jnp.log2(jnp.clip(top, 2.0**-100, 2.0**100)))
+            value = value * jnp.exp2(-column)
             top = jnp.max(jnp.abs(value), axis=1, keepdims=True)
-            exponent = jnp.ceil(jnp.log2(jnp.clip(top, 2.0**-100, 2.0**120)))
-            scaled = value * (jnp.exp2(-exponent) * LEVELS)
+            row = jnp.ceil(jnp.log2(jnp.clip(top, 2.0**-60, 2.0)))
+            scaled = value * (jnp.exp2(-row) * LEVELS)
             scaled = jnp.clip(jnp.round(scaled), -32767.0, 32767.0)
             coded_ref[holder, b * TILE : (b + 1) * TILE, :] = scaled.astype(jnp.int32).astype(jnp.int16)
-            exponents = jnp.where(line == b, to_lanes(exponent), exponents)
+            exponents = jnp.where(line == b, to_lanes(row), exponents)
+            exponents = jnp.where(line == blocks + b, column, exponents)
         coded_ref[holder, blocks * TILE :, :] = exponents.astype(jnp.int32).astype(jnp.int16)
 
 
@@ -104,6 +108,7 @@
         exponents = coded_ref[holder, blocks * TILE :, :].astype(jnp.int32).astype(jnp.float32)
         for b in range(blocks):
             scale = jnp.exp2(to_sublanes(exponents[b : b + 1])) * (1.0 / LEVELS)
+            scale = scale * jnp.exp2(exponents[blocks + b : blocks + b + 1])
             value = coded_ref[holder, b * TILE : (b + 1) * TILE, :].astype(jnp.int32).astype(jnp.float32)
             sums[b] = sums[b] + value * scale
     return jnp.concatenate(sums, axis=0) * root_ref[...]
@@ -242,7 +247,7 @@
 
     mine = requests[0, 0]
     other = lax.ppermute(mine, "row", [(r, r ^ 1) for r in range(row_devices)])
-    pair, copies = lax.optimization_barrier((jnp.concatenate([mine, other]), copies))
+    pair = jnp.concatenate([mine, other])
     tables = [pair]
     for shift in range(1, CHIPS_X):
         tables.append(

time: 265 us -> 265 us (level)
  blocking collectives: 206 us -> 213 us
  waiting for transfers between devices: 9.34 us -> 2.83 us
    all_to_all x1, waiting for transfers between devices: 6.5 us -> 0.01 us  [product(): lax.all_to_all(copies, 'row', split_axis=0, concat_axis=0, tiled=True, ax...]
    all_to_all x1, starting transfers between devices: 3.49 us -> 7.66 us  [product(): lax.all_to_all(copies, 'row', split_axis=0, concat_axis=0, tiled=True, ax...]
    ppermute x1, starting transfers between devices: 12.4 us -> 8.28 us  [on_device(): other = lax.ppermute(mine, 'row', [(r, r ^ 1) for r in range(row_devices)])]
    all_to_all x1, blocking collectives: 16.9 us -> 20.6 us  [product(): lax.all_to_all(copies, 'row', split_axis=0, concat_axis=0, tiled=True, ax...]
  transfers between devices with their start and end apart: 5 -> 5, of which waited for: 2 -> 2; matrix products, arithmetic and copies ran while one was open for 0% -> 1% of each run, Pallas kernels for 0% -> 0%
where the time goes in v5:
time: 265 us
  blocking collectives  213 us (80%)
  starting transfers between devices  23.1 us (9%)
  Pallas kernels  20.2 us (8%)
  waiting for transfers between devices  2.83 us (1%)
    all_to_all x2, blocking collectives, product(): return lax.all_to_all(coded, 'col', split_axis=0, concat_axis=0, tiled=True)  80.3 us
    all_to_all x2, blocking collectives, product(): lax.all_to_all(outgoing, 'row', split_axis=0, concat_axis=0, tiled=True,...  65.8 us
    all_to_all x1, blocking collectives, product(): lax.all_to_all(copies, 'row', split_axis=0, concat_axis=0, tiled=True, ax...  20.6 us
    all_to_all x1, blocking collectives, sum_over_devices(): lax.all_to_all(value.reshape(row_devices, share, width), 'row', split_axi...  18.5 us
    all_to_all x1, blocking collectives, sum_over_devices(): lax.all_to_all(jnp.broadcast_to(part[None], (row_devices, share, width)),...  16 us
    all_to_all x1, blocking collectives, sum_over_devices(): lax.all_to_all(jnp.broadcast_to(part[None], (col_devices, share, width)),...  11.8 us
    pallas_call x1, Pallas kernels, on_device(): call(functools.partial(bases_kernel, scale), (image_shape, image_shape),...  11 us
    ppermute x1, starting transfers between devices, on_device(): other = lax.ppermute(mine, 'row', [(r, r ^ 1) for r in range(row_devices)])  8.28 us
  transfers between devices with their start and end apart: 5, of which 2 were waited for; matrix products, arithmetic and copies ran while one was open for 1% of the time, Pallas kernels for 0%

profile of v5, /device:TPU:1, one launch (start us, length us, event | category | flops | bytes accessed | tf_op | source)
XLA Modules:
  0.0 264.7 jit_solution(15024648717981060910)
XLA Ops:
  0.6 0.0 copy-start.1
  0.6 0.9 copy-done.1
  1.5 0.0 copy-start.2
  1.5 0.7 copy-done.2
  2.2 1.1 shard_map.86
  3.3 7.7 %all-to-all-start = ((bf16[8,256,128]{2,1,0:T(8,128)(2,1)}), bf16[8,256,128]{2,1,0:T(8,128)(2,1)S(1)}, u32[]{:S(2)}, u32[]{:S(2)}) async-start(bf16[8,256,128]{2,1,0:T(8,128)(2,1)} %get-tuple-element.13), calls=%async_computation | async-start | bytes 1048576 | tf_op jit(solution)/shard_map/all_to_all | solution.py:278
  11.0 8.3 %collective-permute-start = (s32[64]{0:T(128)}, s32[64]{0:T(128)S(1)}, u32[]{:S(2)}, u32[]{:S(2)}) collective-permute-start(s32[64]{0:T(128)} %bitcast.21), channel_id=1, source_target_pairs={{0,12},{12,0},{24,36},{36,24},{48,60},{60,48},{72,84},{84,72},{96,... | collective-permute-start | bytes 776 | tf_op jit(solution)/shard_map/ppermute | solution.py:249
  19.9 0.3 collective-permute-done
  20.2 0.7 pad_add_fusion.1
  20.9 1.9 collective-permute-start.3
  22.8 1.9 collective-permute-start.2
  24.8 3.4 %collective-permute-start.1 = (s32[128]{0:T(128)S(1)}, s32[128]{0:T(128)S(1)}, u32[]{:S(2)}, u32[]{:S(2)}) collective-permute-start(s32[128]{0:T(128)S(1)} %pad_add_fusion.1), channel_id=1, source_target_pairs={{0,24},{12,36},{24,48},{36,60},{48,72},{60,84},{72,0},{84,12},{96,... | collective-permute-start | bytes 1544 | tf_op jit(solution)/shard_map/ppermute | solution.py:254
  28.1 0.8 pad_add_fusion.plan
  28.9 0.0 collective-permute-done.3
  28.9 0.0 collective-permute-done.2
  28.9 2.5 collective-permute-done.1
  31.4 0.7 concatenate.14.wanted
  32.2 0.0 all-to-all-done
  32.2 0.7 shard_map.87
  32.9 0.0 copy-start
  32.9 31.6 %all_to_all.45 = bf16[8,8,128,128]{3,2,1,0:T(8,128)(2,1)S(1)} all-to-all(bf16[8,8,128,128]{3,2,1,0:T(8,128)(2,1)S(1)} %shard_map.87), channel_id=1, replica_groups={{0,12,24,36,48,60,72,84},{96,108,120,132,144,156,168,180},{192,204,216,..., dimensions={0} | all-to-all | bytes 4194304 | tf_op jit(solution)/shard_map/all_to_all | solution.py:282
  64.5 0.0 copy-done
  64.5 2.5 shard_map.88
  67.0 42.0 %all_to_all.46.coded_ref = s16[12,272,128]{2,1,0:T(8,128)(2,1)S(1)} all-to-all(s16[12,272,128]{2,1,0:T(8,128)(2,1)S(1)} %shard_map.88), channel_id=1, replica_groups=mesh['row'=64,'col'=12] {'col'}, dimensions={0} | all-to-all | bytes 1671168 | tf_op jit(solution)/shard_map/all_to_all | solution.py:286
  109.0 0.8 shard_map.89
  109.8 20.6 %all_to_all.47 = bf16[8,256,128]{2,1,0:T(8,128)(2,1)S(1)} all-to-all(bf16[8,256,128]{2,1,0:T(8,128)(2,1)S(1)} %get-tuple-element.16), channel_id=1, replica_groups={{0,96,192,288,384,480,576,672},{12,108,204,300,396,492,588,684},{24,120..., dimensions={0} | all-to-all | bytes 1048576 | tf_op jit(solution)/shard_map/all_to_all | solution.py:278
  130.4 0.7 shard_map.90
  131.2 34.3 %all_to_all.48 = bf16[8,8,128,128]{3,2,1,0:T(8,128)(2,1)S(1)} all-to-all(bf16[8,8,128,128]{3,2,1,0:T(8,128)(2,1)S(1)} %shard_map.90), channel_id=1, replica_groups={{0,12,24,36,48,60,72,84},{96,108,120,132,144,156,168,180},{192,204,216,..., dimensions={0} | all-to-all | bytes 4194304 | tf_op jit(solution)/shard_map/all_to_all | solution.py:282
  165.4 2.5 shard_map.91
  168.0 38.3 %all_to_all.49.coded_ref = s16[12,272,128]{2,1,0:T(8,128)(2,1)S(1)} all-to-all(s16[12,272,128]{2,1,0:T(8,128)(2,1)S(1)} %shard_map.91), channel_id=1, replica_groups=mesh['row'=64,'col'=12] {'col'}, dimensions={0} | all-to-all | bytes 1671168 | tf_op jit(solution)/shard_map/all_to_all | solution.py:286
  206.3 0.8 shard_map.92
  207.1 0.1 reshape.36
  207.2 18.5 %all_to_all.50 = f32[64,2,256]{2,1,0:T(2,128)S(1)} all-to-all(f32[64,2,256]{2,1,0:T(2,128)S(1)} %reshape.36), channel_id=1, replica_groups=mesh['row'=64,'col'=12] {'row'}, dimensions={0} | all-to-all | bytes 262144 | tf_op jit(solution)/shard_map/all_to_all | solution.py:211
  225.7 0.1 reduce_sum.18
  225.8 11.8 %all_to_all.51 = f32[12,2,256]{2,1,0:T(2,128)S(1)} all-to-all(f32[12,2,256]{2,1,0:T(2,128)S(1)} %broadcast_in_dim.4), channel_id=1, replica_groups=mesh['row'=64,'col'=12] {'col'}, dimensions={0} | all-to-all | bytes 49152 | tf_op jit(solution)/shard_map/all_to_all | solution.py:215
  237.6 16.0 %all_to_all.52 = f32[64,2,256]{2,1,0:T(2,128)S(1)} all-to-all(f32[64,2,256]{2,1,0:T(2,128)S(1)} %broadcast_in_dim.5), channel_id=1, replica_groups=mesh['row'=64,'col'=12] {'row'}, dimensions={0} | all-to-all | bytes 262144 | tf_op jit(solution)/shard_map/all_to_all | solution.py:219
  253.7 0.1 reshape.37.grams_ref
  253.8 11.0 %shard_map.93 = (f32[256,128]{1,0:T(8,128)}, f32[256,128]{1,0:T(8,128)}) custom-call(f32[128,256]{1,0:T(8,128)S(1)} %reshape.37.grams_ref, f32[256,128]{1,0:T(8,128)S(1)} %get-tuple-element.18.image_one_ref, f32[256,128]{1,0:T(8,128)S(1)} %get-tuple-element.19.image_two_ref), custom_call_target="tpu_custom_call" | custom-call | tf_op jit(solution)/shard_map/pallas_call | solution.py:297
  (4 shorter events, 0.1 us)
Async XLA Ops:
  0.6 0.9 copy-start.1
  1.5 0.7 copy-start.2
  3.3 28.9 %all-to-all-start = ((bf16[8,256,128]{2,1,0:T(8,128)(2,1)}), bf16[8,256,128]{2,1,0:T(8,128)(2,1)S(1)}, u32[]{:S(2)}, u32[]{:S(2)}) async-start(bf16[8,256,128]{2,1,0:T(8,128)(2,1)} %get-tuple-element.13), calls=%async_computation | async-start | bytes 1048576 | tf_op jit(solution)/shard_map/all_to_all | solution.py:278
  11.0 9.2 %collective-permute-start = (s32[64]{0:T(128)}, s32[64]{0:T(128)S(1)}, u32[]{:S(2)}, u32[]{:S(2)}) collective-permute-start(s32[64]{0:T(128)} %bitcast.21), channel_id=1, source_target_pairs={{0,12},{12,0},{24,36},{36,24},{48,60},{60,48},{72,84},{84,72},{96,... | collective-permute-start | bytes 776 | tf_op jit(solution)/shard_map/ppermute | solution.py:249
  20.9 8.0 %collective-permute-start.3 = (s32[128]{0:T(128)S(1)}, s32[128]{0:T(128)S(1)}, u32[]{:S(2)}, u32[]{:S(2)}) collective-permute-start(s32[128]{0:T(128)S(1)} %pad_add_fusion.1), channel_id=1, source_target_pairs={{0,72},{12,84},{24,0},{36,12},{48,24},{60,36},{72,48},{84,60},{96,... | collective-permute-start | bytes 1544 | tf_op jit(solution)/shard_map/ppermute | solution.py:254
  22.8 6.1 %collective-permute-start.2 = (s32[128]{0:T(128)S(1)}, s32[128]{0:T(128)S(1)}, u32[]{:S(2)}, u32[]{:S(2)}) collective-permute-start(s32[128]{0:T(128)S(1)} %pad_add_fusion.1), channel_id=1, source_target_pairs={{0,48},{12,60},{24,72},{36,84},{48,0},{60,12},{72,24},{84,36},{96,... | collective-permute-start | bytes 1544 | tf_op jit(solution)/shard_map/ppermute | solution.py:254
  24.8 6.7 %collective-permute-start.1 = (s32[128]{0:T(128)S(1)}, s32[128]{0:T(128)S(1)}, u32[]{:S(2)}, u32[]{:S(2)}) collective-permute-start(s32[128]{0:T(128)S(1)} %pad_add_fusion.1), channel_id=1, source_target_pairs={{0,24},{12,36},{24,48},{36,60},{48,72},{60,84},{72,0},{84,12},{96,... | collective-permute-start | bytes 1544 | tf_op jit(solution)/shard_map/ppermute | solution.py:254
  32.9 31.6 %copy-start = (bf16[1,1,96,128,128]{4,3,2,1,0:T(8,128)(2,1)S(1)}, bf16[1,1,96,128,128]{4,3,2,1,0:T(8,128)(2,1)}, u32[]{:S(2)}) copy-start(bf16[1,1,96,128,128]{4,3,2,1,0:T(8,128)(2,1)} %param.9) | copy-start | bytes 9437188

commit v6 on v4

--- a/solution.py
+++ b/solution.py
@@ -87,12 +87,16 @@
         exponents = jnp.zeros((EXTRA, TILE), jnp.float32)
         for b in range(blocks):
             value = total[holder * blocks + b]
+            top = jnp.max(jnp.abs(value), axis=0, keepdims=True)
+            column = jnp.ceil(jnp.log2(jnp.clip(top, 2.0**-100, 2.0**100)))
+            value = value * jnp.exp2(-column)
             top = jnp.max(jnp.abs(value), axis=1, keepdims=True)
-            exponent = jnp.ceil(jnp.log2(jnp.clip(top, 2.0**-100, 2.0**120)))
-            scaled = value * (jnp.exp2(-exponent) * LEVELS)
+            row = jnp.ceil(jnp.log2(jnp.clip(top, 2.0**-60, 2.0)))
+            scaled = value * (jnp.exp2(-row) * LEVELS)
             scaled = jnp.clip(jnp.round(scaled), -32767.0, 32767.0)
             coded_ref[holder, b * TILE : (b + 1) * TILE, :] = scaled.astype(jnp.int32).astype(jnp.int16)
-            exponents = jnp.where(line == b, to_lanes(exponent), exponents)
+            exponents = jnp.where(line == b, to_lanes(row), exponents)
+            exponents = jnp.where(line == blocks + b, column, exponents)
         coded_ref[holder, blocks * TILE :, :] = exponents.astype(jnp.int32).astype(jnp.int16)
 
 
@@ -104,6 +108,7 @@
         exponents = coded_ref[holder, blocks * TILE :, :].astype(jnp.int32).astype(jnp.float32)
         for b in range(blocks):
             scale = jnp.exp2(to_sublanes(exponents[b : b + 1])) * (1.0 / LEVELS)
+            scale = scale * jnp.exp2(exponents[blocks + b : blocks + b + 1])
             value = coded_ref[holder, b * TILE : (b + 1) * TILE, :].astype(jnp.int32).astype(jnp.float32)
             sums[b] = sums[b] + value * scale
     return jnp.concatenate(sums, axis=0) * root_ref[...]
@@ -134,6 +139,8 @@
 
 def inverse_cholesky(gram):
     size = gram.shape[0]
+    unit = lax.rsqrt(jnp.sum(jnp.where(diagonal_mask(), gram, 0.0), axis=0, keepdims=True))
+    gram = gram * unit * to_sublanes(unit)
     band = (SUBLANES, size)
     lane = lax.broadcasted_iota(jnp.int32, band, 1)
     line = lax.broadcasted_iota(jnp.int32, band, 0)
@@ -185,7 +192,7 @@
             while len(terms) > 1:
                 terms = [terms[i] + terms[i + 1] for i in range(0, len(terms), 2)]
             left[q] = jnp.where(cleared, 0.0, left[q]) - terms[0]
-    return jnp.concatenate(result, axis=0)
+    return jnp.concatenate(result, axis=0) * unit
 
 
 def bases_kernel(scale, grams_ref, image_one_ref, image_two_ref, first_ref, second_ref):

time: 264 us -> 265 us (level)
    all_to_all x2, blocking collectives: 78.6 us -> 81.4 us  [product(): return lax.all_to_all(coded, 'col', split_axis=0, concat_axis=0, tiled=True)]
where the time goes in v6:
time: 265 us; the launch traced here: 264 us
  blocking collectives  214 us (81%)
  starting transfers between devices  23.1 us (9%)
  Pallas kernels  19.5 us (7%)
  waiting for transfers between devices  2.83 us (1%)
    all_to_all x2, blocking collectives, product(): return lax.all_to_all(coded, 'col', split_axis=0, concat_axis=0, tiled=True)  81.4 us
    all_to_all x2, blocking collectives, product(): lax.all_to_all(outgoing, 'row', split_axis=0, concat_axis=0, tiled=True,...  67 us
    all_to_all x1, blocking collectives, product(): lax.all_to_all(copies, 'row', split_axis=0, concat_axis=0, tiled=True, ax...  19 us
    all_to_all x1, blocking collectives, sum_over_devices(): lax.all_to_all(value.reshape(row_devices, share, width), 'row', split_axi...  18.4 us
    all_to_all x1, blocking collectives, sum_over_devices(): lax.all_to_all(jnp.broadcast_to(part[None], (row_devices, share, width)),...  16 us
    all_to_all x1, blocking collectives, sum_over_devices(): lax.all_to_all(jnp.broadcast_to(part[None], (col_devices, share, width)),...  11.8 us
    pallas_call x1, Pallas kernels, on_device(): call(functools.partial(bases_kernel, scale), (image_shape, image_shape),...  10.3 us
    ppermute x1, starting transfers between devices, on_device(): other = lax.ppermute(mine, 'row', [(r, r ^ 1) for r in range(row_devices)])  8.28 us
  transfers between devices with their start and end apart: 5, of which 2 were waited for; matrix products, arithmetic and copies ran while one was open for 1% of the time, Pallas kernels for 0%

profile of v6, /device:TPU:1, one launch (start us, length us, event | category | flops | bytes accessed | tf_op | source)
XLA Modules:
  0.0 264.5 jit_solution(4770345840533603235)
XLA Ops:
  0.6 0.0 copy-start.1
  0.6 0.9 copy-done.1
  1.5 0.0 copy-start.2
  1.5 0.7 copy-done.2
  2.2 1.1 shard_map.86
  3.3 7.7 %all-to-all-start = ((bf16[8,256,128]{2,1,0:T(8,128)(2,1)}), bf16[8,256,128]{2,1,0:T(8,128)(2,1)S(1)}, u32[]{:S(2)}, u32[]{:S(2)}) async-start(bf16[8,256,128]{2,1,0:T(8,128)(2,1)} %get-tuple-element.13), calls=%async_computation | async-start | bytes 1048576 | tf_op jit(solution)/shard_map/all_to_all | solution.py:294
  11.0 8.3 %collective-permute-start = (s32[64]{0:T(128)}, s32[64]{0:T(128)S(1)}, u32[]{:S(2)}, u32[]{:S(2)}) collective-permute-start(s32[64]{0:T(128)} %bitcast.21), channel_id=1, source_target_pairs={{0,12},{12,0},{24,36},{36,24},{48,60},{60,48},{72,84},{84,72},{96,... | collective-permute-start | bytes 776 | tf_op jit(solution)/shard_map/ppermute | solution.py:265
  19.9 0.3 collective-permute-done
  20.2 0.7 pad_add_fusion.1
  20.9 1.9 collective-permute-start.3
  22.8 1.9 collective-permute-start.2
  24.8 3.4 %collective-permute-start.1 = (s32[128]{0:T(128)S(1)}, s32[128]{0:T(128)S(1)}, u32[]{:S(2)}, u32[]{:S(2)}) collective-permute-start(s32[128]{0:T(128)S(1)} %pad_add_fusion.1), channel_id=1, source_target_pairs={{0,24},{12,36},{24,48},{36,60},{48,72},{60,84},{72,0},{84,12},{96,... | collective-permute-start | bytes 1544 | tf_op jit(solution)/shard_map/ppermute | solution.py:270
  28.1 0.8 pad_add_fusion.plan
  28.9 0.0 collective-permute-done.3
  28.9 0.0 collective-permute-done.2
  28.9 2.5 collective-permute-done.1
  31.4 0.7 concatenate.14.wanted
  32.2 0.0 all-to-all-done
  32.2 0.7 shard_map.87
  32.9 0.0 copy-start
  32.9 31.6 %all_to_all.45 = bf16[8,8,128,128]{3,2,1,0:T(8,128)(2,1)S(1)} all-to-all(bf16[8,8,128,128]{3,2,1,0:T(8,128)(2,1)S(1)} %shard_map.87), channel_id=1, replica_groups={{0,12,24,36,48,60,72,84},{96,108,120,132,144,156,168,180},{192,204,216,..., dimensions={0} | all-to-all | bytes 4194304 | tf_op jit(solution)/shard_map/all_to_all | solution.py:298
  64.5 0.0 copy-done
  64.5 2.5 shard_map.88
  67.0 44.0 %all_to_all.46.coded_ref = s16[12,272,128]{2,1,0:T(8,128)(2,1)S(1)} all-to-all(s16[12,272,128]{2,1,0:T(8,128)(2,1)S(1)} %shard_map.88), channel_id=1, replica_groups=mesh['row'=64,'col'=12] {'col'}, dimensions={0} | all-to-all | bytes 1671168 | tf_op jit(solution)/shard_map/all_to_all | solution.py:302
  111.1 0.8 shard_map.89
  111.9 19.0 %all_to_all.47 = bf16[8,256,128]{2,1,0:T(8,128)(2,1)S(1)} all-to-all(bf16[8,256,128]{2,1,0:T(8,128)(2,1)S(1)} %get-tuple-element.16), channel_id=1, replica_groups={{0,96,192,288,384,480,576,672},{12,108,204,300,396,492,588,684},{24,120..., dimensions={0} | all-to-all | bytes 1048576 | tf_op jit(solution)/shard_map/all_to_all | solution.py:294
  130.8 0.7 shard_map.90
  131.6 35.4 %all_to_all.48 = bf16[8,8,128,128]{3,2,1,0:T(8,128)(2,1)S(1)} all-to-all(bf16[8,8,128,128]{3,2,1,0:T(8,128)(2,1)S(1)} %shard_map.90), channel_id=1, replica_groups={{0,12,24,36,48,60,72,84},{96,108,120,132,144,156,168,180},{192,204,216,..., dimensions={0} | all-to-all | bytes 4194304 | tf_op jit(solution)/shard_map/all_to_all | solution.py:298
  167.0 2.5 shard_map.91
  169.5 37.3 %all_to_all.49.coded_ref = s16[12,272,128]{2,1,0:T(8,128)(2,1)S(1)} all-to-all(s16[12,272,128]{2,1,0:T(8,128)(2,1)S(1)} %shard_map.91), channel_id=1, replica_groups=mesh['row'=64,'col'=12] {'col'}, dimensions={0} | all-to-all | bytes 1671168 | tf_op jit(solution)/shard_map/all_to_all | solution.py:302
  206.8 0.8 shard_map.92
  207.6 0.1 reshape.36
  207.7 18.4 %all_to_all.50 = f32[64,2,256]{2,1,0:T(2,128)S(1)} all-to-all(f32[64,2,256]{2,1,0:T(2,128)S(1)} %reshape.36), channel_id=1, replica_groups=mesh['row'=64,'col'=12] {'row'}, dimensions={0} | all-to-all | bytes 262144 | tf_op jit(solution)/shard_map/all_to_all | solution.py:227
  226.1 0.1 reduce_sum.18
  226.2 11.8 %all_to_all.51 = f32[12,2,256]{2,1,0:T(2,128)S(1)} all-to-all(f32[12,2,256]{2,1,0:T(2,128)S(1)} %broadcast_in_dim.4), channel_id=1, replica_groups=mesh['row'=64,'col'=12] {'col'}, dimensions={0} | all-to-all | bytes 49152 | tf_op jit(solution)/shard_map/all_to_all | solution.py:231
  238.1 16.0 %all_to_all.52 = f32[64,2,256]{2,1,0:T(2,128)S(1)} all-to-all(f32[64,2,256]{2,1,0:T(2,128)S(1)} %broadcast_in_dim.5), channel_id=1, replica_groups=mesh['row'=64,'col'=12] {'row'}, dimensions={0} | all-to-all | bytes 262144 | tf_op jit(solution)/shard_map/all_to_all | solution.py:235
  254.1 0.1 reshape.37.grams_ref
  254.2 10.3 %shard_map.93 = (f32[256,128]{1,0:T(8,128)}, f32[256,128]{1,0:T(8,128)}) custom-call(f32[128,256]{1,0:T(8,128)S(1)} %reshape.37.grams_ref, f32[256,128]{1,0:T(8,128)S(1)} %get-tuple-element.18.image_one_ref, f32[256,128]{1,0:T(8,128)S(1)} %get-tuple-element.19.image_two_ref), custom_call_target="tpu_custom_call" | custom-call | tf_op jit(solution)/shard_map/pallas_call | solution.py:313
  (4 shorter events, 0.1 us)
Async XLA Ops:
  0.6 0.9 copy-start.1
  1.5 0.7 copy-start.2
  3.3 28.9 %all-to-all-start = ((bf16[8,256,128]{2,1,0:T(8,128)(2,1)}), bf16[8,256,128]{2,1,0:T(8,128)(2,1)S(1)}, u32[]{:S(2)}, u32[]{:S(2)}) async-start(bf16[8,256,128]{2,1,0:T(8,128)(2,1)} %get-tuple-element.13), calls=%async_computation | async-start | bytes 1048576 | tf_op jit(solution)/shard_map/all_to_all | solution.py:294
  11.0 9.2 %collective-permute-start = (s32[64]{0:T(128)}, s32[64]{0:T(128)S(1)}, u32[]{:S(2)}, u32[]{:S(2)}) collective-permute-start(s32[64]{0:T(128)} %bitcast.21), channel_id=1, source_target_pairs={{0,12},{12,0},{24,36},{36,24},{48,60},{60,48},{72,84},{84,72},{96,... | collective-permute-start | bytes 776 | tf_op jit(solution)/shard_map/ppermute | solution.py:265
  20.9 8.0 %collective-permute-start.3 = (s32[128]{0:T(128)S(1)}, s32[128]{0:T(128)S(1)}, u32[]{:S(2)}, u32[]{:S(2)}) collective-permute-start(s32[128]{0:T(128)S(1)} %pad_add_fusion.1), channel_id=1, source_target_pairs={{0,72},{12,84},{24,0},{36,12},{48,24},{60,36},{72,48},{84,60},{96,... | collective-permute-start | bytes 1544 | tf_op jit(solution)/shard_map/ppermute | solution.py:270
  22.8 6.1 %collective-permute-start.2 = (s32[128]{0:T(128)S(1)}, s32[128]{0:T(128)S(1)}, u32[]{:S(2)}, u32[]{:S(2)}) collective-permute-start(s32[128]{0:T(128)S(1)} %pad_add_fusion.1), channel_id=1, source_target_pairs={{0,48},{12,60},{24,72},{36,84},{48,0},{60,12},{72,24},{84,36},{96,... | collective-permute-start | bytes 1544 | tf_op jit(solution)/shard_map/ppermute | solution.py:270
  24.8 6.7 %collective-permute-start.1 = (s32[128]{0:T(128)S(1)}, s32[128]{0:T(128)S(1)}, u32[]{:S(2)}, u32[]{:S(2)}) collective-permute-start(s32[128]{0:T(128)S(1)} %pad_add_fusion.1), channel_id=1, source_target_pairs={{0,24},{12,36},{24,48},{36,60},{48,72},{60,84},{72,0},{84,12},{96,... | collective-permute-start | bytes 1544 | tf_op jit(solution)/shard_map/ppermute | solution.py:270
  32.9 31.6 %copy-start = (bf16[1,1,96,128,128]{4,3,2,1,0:T(8,128)(2,1)S(1)}, bf16[1,1,96,128,128]{4,3,2,1,0:T(8,128)(2,1)}, u32[]{:S(2)}) copy-start(bf16[1,1,96,128,128]{4,3,2,1,0:T(8,128)(2,1)} %param.9) | copy-start | bytes 9437188
